TPU v7x, 512 devices: a whole 4x4x16 slice. The times are simulated.
512 devices in a mesh: gx: 8 (over x, core), gy: 16 (over z), gz: 4 (over y).
Axes of the slice: x: 4, y: 4, z: 16, core: 2. Of those that a mesh axis runs over, the one named last changes fastest.
Arguments:
- gradient: bfloat16 [8, 2048, 8192], P('gx', ('gy', 'gz')), may hold values from -1000 to 1000, as said below
- error_buffer: bfloat16 [8, 2048, 8192], P('gx', ('gy', 'gz')), may hold values from -6 to 6
- warm_factor: float32 [32, 2048], P(None, ('gy', 'gz')), may hold values from -6 to 6
Outputs:
- applied_update: bfloat16 [2048, 8192], P(('gy', 'gz'))
- next_error: bfloat16 [8, 2048, 8192], P('gx', ('gy', 'gz'))
- next_factor: float32 [32, 2048], P(None, ('gy', 'gz'))
Inputs may be any that keep to these rules, and one draw needn't show every extreme that they name: Real-valued gradient entries.
All inputs are finite; a program needn't handle non-finite values.
Results may differ from a plain program's by a relative error of at most 0.012.
Values may be sent and summed in bfloat16 or wider, within the bound.
No kernel may reach another device: no remote copies, remote signals or barrier semaphores. Data moves between devices by JAX's collectives and lax.ppermute only.
A program may use at most 64 MiB of HBM per device.

v0:
```python
import math

import jax
import jax.numpy as jnp
from jax import lax
from jax.sharding import PartitionSpec as P


def lower_factor(gram_matrix):
    rank_dim = gram_matrix.shape[0]
    ridge_term = 0.0001 * jnp.trace(gram_matrix) / rank_dim
    return jnp.linalg.cholesky(
        gram_matrix + ridge_term * jnp.eye(rank_dim, dtype=gram_matrix.dtype)
    )


def per_device(gradient, error_buffer, warm_factor):
    merged = (gradient[0].astype(jnp.float32) + error_buffer[0].astype(jnp.float32)).astype(
        jnp.bfloat16
    )
    replicas = lax.axis_size("gx")
    col_width = merged.shape[0]
    row_count = merged.shape[1]
    all_cols = col_width * lax.axis_size("gy") * lax.axis_size("gz")
    partial_rows = jnp.dot(
        warm_factor.astype(jnp.bfloat16), merged, preferred_element_type=jnp.float32
    )
    row_factor = lax.psum(partial_rows, ("gx", "gy", "gz")) / replicas
    gram_matrix = jnp.dot(row_factor, row_factor.T, precision=lax.Precision.HIGHEST)
    lower = lower_factor(gram_matrix)
    basis = lax.linalg.triangular_solve(lower, row_factor, left_side=True, lower=True).astype(
        jnp.bfloat16
    )
    column_part = lax.dot_general(
        basis, merged, (((1,), (1,)), ((), ())), preferred_element_type=jnp.float32
    )
    next_factor = lax.psum(column_part, "gx") / replicas
    norm_sq = lax.psum(jnp.sum(next_factor * next_factor), ("gy", "gz"))
    norm_limit = 0.1 * math.sqrt(all_cols * row_count)
    clip_scale = jnp.minimum(1.0, norm_limit / jnp.sqrt(norm_sq + 1e-06))
    decompressed = lax.dot_general(
        next_factor.astype(jnp.bfloat16),
        basis,
        (((0,), (0,)), ((), ())),
        preferred_element_type=jnp.float32,
    )
    applied_update = (clip_scale * decompressed).astype(jnp.bfloat16)
    next_error = (merged.astype(jnp.float32) - decompressed).astype(jnp.bfloat16)[None]
    return (applied_update, next_error, next_factor)


def solution(mesh):
    in_specs = (P("gx", ("gy", "gz"), None), P("gx", ("gy", "gz"), None), P(None, ("gy", "gz")))
    out_specs = (P(("gy", "gz"), None), P("gx", ("gy", "gz"), None), P(None, ("gy", "gz")))
    return jax.shard_map(
        per_device, mesh=mesh, in_specs=in_specs, out_specs=out_specs, check_vma=False
    )
```

profile of v0, /device:TPU:8, one launch (start us, length us, event | category | flops | bytes accessed | tf_op | source)
XLA Modules:
  0.0 670.9 jit_solution(17880128978457003595)
XLA Ops:
  7.2 0.0 all-reduce.2.cloned.1.call-start
  7.2 2.5 convolution_bitcast_fusion
  9.8 0.0 all-reduce.2.cloned.1.call-update
  9.8 474.5 %all-reduce.2.cloned.1.call-done = f32[32,8192]{1,0:T(8,128)} async-done(((f32[32,8192]{1,0:T(8,128)}), f32[32,8192]{1,0:T(8,128)}) %all-reduce.2.cloned.1.call-update) | async-done | bytes 1048592 | tf_op jit(solution)/shard_map/psum | solution.py:28
  484.3 0.0 copy-start.2
  484.3 3.3 select_reduce_fusion.1
  487.5 0.1 copy.6
  488.3 2.9 cholesky.17
  491.2 0.6 compare_reduce_fusion
  491.9 0.7 fusion.7
  492.5 2.4 custom-call.6
  495.0 0.0 copy-done.2
  495.0 0.0 copy-start
  495.0 0.0 copy-start.1
  495.0 1.0 convolution_convert_fusion
  496.0 0.0 copy-done
  496.0 0.2 copy-done.1
  496.2 0.3 fusion.16
  496.5 25.7 %psum.22 = f32[32,32]{1,0:T(8,128)S(1)} all-reduce(f32[32,32]{1,0:T(8,128)S(1)} %fusion.16), channel_id=1, replica_groups=mesh['gx'=8,'gy'=16,'gz'=4] {'gx'}, use_global_device_ids=true, to_apply=%region_4.5 | all-reduce | flops 1024 | bytes 8192 | tf_op jit(solution)/shard_map/psum | solution.py:37
  522.2 0.6 multiply_reduce_fusion
  522.8 0.0 copy-start.3
  522.8 139.2 %psum.23 = f32[]{:T(128)} all-reduce(f32[]{:T(128)} %get-tuple-element.3), channel_id=1, replica_groups=mesh['gx'=8,'gy'=16,'gz'=4] {'gy','gz'}, use_global_device_ids=true, to_apply=%region_6.7 | all-reduce | flops 1 | bytes 8 | tf_op jit(solution)/shard_map/psum | solution.py:38
  662.7 1.3 fusion.4
  664.1 0.0 copy-done.3
  (2 shorter events, 0.0 us)
Async XLA Ops:
  7.2 477.1 %all-reduce.2.cloned.1.call-start = ((), (), s32[]{:S(2)}) async-start(), calls=%async_computation | async-start | bytes 2097152 | tf_op jit(solution)/shard_map/psum | solution.py:28
  484.3 10.7 %copy-start.2 = (f32[32,8192]{1,0:T(8,128)S(1)}, f32[32,8192]{1,0:T(8,128)}, u32[]{:S(2)}) copy-start(f32[32,8192]{1,0:T(8,128)} %all-reduce.2.cloned.1.call-done) | copy-start | bytes 3145732
  495.0 1.1 copy-start
  495.0 1.2 copy-start.1
  522.8 141.2 %copy-start.3 = (f32[32,32]{1,0:T(8,128)}, f32[32,32]{1,0:T(8,128)S(1)}, u32[]{:S(2)}) copy-start(f32[32,32]{1,0:T(8,128)S(1)} %get-tuple-element.4) | copy-start | bytes 12292
Sparse Core Ops, SparseCore 0:
  13.4 470.7 all-reduce.1
where the time goes:
time: 671 us
  waiting for transfers between devices  474 us (71%)
  blocking collectives  165 us (25%)
  between operations  15.4 us (2%)
  matrix products  8.43 us (1%)
  other arithmetic  7.29 us (1%)
    psum x1, waiting for transfers between devices, per_device(): row_factor = lax.psum(partial_rows, ('gx', 'gy', 'gz')) / replicas  474 us
    psum x1, blocking collectives, per_device(): norm_sq = lax.psum(jnp.sum(next_factor * next_factor), ('gy', 'gz'))  139 us
    psum x1, blocking collectives, per_device(): next_factor = lax.psum(column_part, 'gx') / replicas  25.7 us
  transfers between devices with their start and end apart: 1, of which 1 were waited for; matrix products, arithmetic and copies ran while one was open for 0% of the time, Pallas kernels for 0%

commit v1 on v0

v1 whole, which is shorter than its diff:
```python
import math

import jax
import jax.numpy as jnp
from jax import lax
from jax.experimental import pallas as pl
from jax.experimental.pallas import tpu as pltpu
from jax.sharding import PartitionSpec as P

F32 = jnp.float32
BF16 = jnp.bfloat16
HIGHEST = lax.Precision.HIGHEST
PARAMS = pltpu.CompilerParams(vmem_limit_bytes=16 * 1024 * 1024)


def split3(value):
    high = value.astype(BF16)
    rest = value - high.astype(F32)
    middle = rest.astype(BF16)
    low = (rest - middle.astype(F32)).astype(BF16)
    return high, middle, low


def merge_kernel(gradient_ref, error_ref, warm_ref, send_ref):
    peers, half, _ = send_ref.shape
    chunk = gradient_ref.shape[1] // peers
    rank, width = warm_ref.shape
    warm = warm_ref[...].astype(BF16)
    packed = jnp.concatenate(
        [warm[:half], warm[half:], jnp.zeros((half, 128 - 2 * width), BF16)], axis=1
    )
    for peer in range(peers):
        part = slice(peer * chunk, (peer + 1) * chunk)
        tile = (gradient_ref[:, part].astype(F32) + error_ref[:, part].astype(F32)).astype(BF16)
        send_ref[peer, :, 0:chunk] = tile[:half]
        send_ref[peer, :, chunk : 2 * chunk] = tile[half:]
        send_ref[peer, :, 2 * chunk :] = packed


def rows_kernel(groups, width, scale, got_ref, mean_ref, send_ref):
    peers, half, wide = got_ref.shape
    chunk = (wide - 128) // 2
    replicas = peers // groups
    warm = []
    for group in range(groups):
        total = got_ref[group, :, 0 : 2 * chunk].astype(F32)
        for replica in range(1, replicas):
            total += got_ref[replica * groups + group, :, 0 : 2 * chunk].astype(F32)
        total *= scale
        top = group * 2 * half
        mean_ref[top : top + half, :] = total[:, :chunk]
        mean_ref[top + half : top + 2 * half, :] = total[:, chunk:]
        packed = got_ref[group, :, 2 * chunk :].astype(F32)
        warm.append(jnp.concatenate([packed[:, :width], packed[:, width : 2 * width]], axis=0))
    rows = jnp.dot(
        jnp.concatenate(warm, axis=1), mean_ref[...], precision=HIGHEST, preferred_element_type=F32
    ).astype(BF16)
    for peer in range(send_ref.shape[0]):
        send_ref[peer] = rows


def columns_kernel(groups, got_ref, mean_ref, send_ref):
    peers, rank, chunk = got_ref.shape
    total = got_ref[0].astype(F32)
    for peer in range(1, peers):
        total += got_ref[peer].astype(F32)
    rows = total.astype(BF16)
    product = lax.dot_general(
        rows.astype(F32),
        mean_ref[...],
        (((1,), (1,)), ((), ())),
        precision=HIGHEST,
        preferred_element_type=F32,
    )
    width = product.shape[1] // groups
    for group in range(groups):
        pieces = split3(product[:, group * width : (group + 1) * width])
        pad = jnp.zeros((rank, 128 - 3 * width), BF16)
        tail = jnp.concatenate([*pieces, pad], axis=1)
        for replica in range(send_ref.shape[0] // groups):
            send_ref[replica * groups + group, :, 0:chunk] = rows
            send_ref[replica * groups + group, :, chunk:] = tail


def factor_kernel(got_ref, rows_ref, next_ref, mix_ref, norm_ref):
    peers, rank, wide = got_ref.shape
    chunk = wide - 128
    width = next_ref.shape[1]
    tails = got_ref[0, :, chunk:].astype(F32)
    for peer in range(1, peers):
        tails += got_ref[peer, :, chunk:].astype(F32)
    product = tails[:, :width] + tails[:, width : 2 * width] + tails[:, 2 * width : 3 * width]
    for peer in range(peers):
        rows_ref[:, peer * chunk : (peer + 1) * chunk] = got_ref[peer, :, 0:chunk]
    rows = rows_ref[...]
    gram = lax.dot_general(rows, rows, (((1,), (1,)), ((), ())), preferred_element_type=F32)
    line = lax.broadcasted_iota(jnp.int32, (rank, rank), 0)
    eye = (line == lax.broadcasted_iota(jnp.int32, (rank, rank), 1)).astype(F32)
    trace = jnp.sum(gram * eye)
    gram = gram + (0.0001 * trace / rank) * eye
    work = jnp.concatenate([gram, product, eye], axis=1)
    line = lax.broadcasted_iota(jnp.int32, work.shape, 0)
    for step in range(rank):
        pivot_row = work[step : step + 1, :]
        scaled = pivot_row * lax.rsqrt(pivot_row[:, step : step + 1])
        column = work[:, step : step + 1] * lax.rsqrt(pivot_row[:, step : step + 1])
        work = jnp.where(line > step, work - column * scaled, jnp.where(line == step, scaled, work))
    next_factor = work[:, rank : rank + width]
    inverse = work[:, rank + width :]
    next_ref[...] = next_factor
    norm_ref[...] = jnp.full(norm_ref.shape, jnp.sum(next_factor * next_factor), F32)
    mix = lax.dot_general(
        next_factor,
        inverse,
        (((0,), (0,)), ((), ())),
        precision=HIGHEST,
        preferred_element_type=F32,
    )
    mix_ref[...] = jnp.concatenate([*split3(mix), jnp.zeros((width, 128 - 3 * rank), BF16)], axis=1)


def update_kernel(norm_limit, norms_ref, mix_ref, rows_ref, gradient_ref, error_ref, applied_ref, next_ref):
    rank, row_count = rows_ref.shape
    norm_sq = jnp.sum(norms_ref[...][:, 0:1])
    clip_scale = jnp.minimum(1.0, norm_limit * lax.rsqrt(jnp.full((1, 1), norm_sq + 1e-06, F32)))
    mix = mix_ref[...][:, : 3 * rank]
    step = 1024
    for start in range(0, row_count, step):
        part = slice(start, start + step)
        rows = rows_ref[:, part]
        decompressed = jnp.dot(
            mix, jnp.concatenate([rows, rows, rows], axis=0), preferred_element_type=F32
        )
        applied_ref[:, part] = (clip_scale * decompressed).astype(BF16)
        tile = (gradient_ref[:, part].astype(F32) + error_ref[:, part].astype(F32)).astype(BF16)
        next_ref[:, part] = (tile.astype(F32) - decompressed).astype(BF16)


def call(kernel, outs, *args):
    return pl.pallas_call(
        kernel,
        out_shape=outs,
        in_specs=[pl.BlockSpec(memory_space=pltpu.VMEM)] * len(args),
        out_specs=jax.tree.map(lambda _: pl.BlockSpec(memory_space=pltpu.VMEM), outs),
        compiler_params=PARAMS,
    )(*args)


def per_device(gradient, error_buffer, warm_factor):
    shape = jax.ShapeDtypeStruct
    replicas, depth, groups = (lax.axis_size(axis) for axis in ("gx", "gy", "gz"))
    gradient, error_buffer = gradient[0], error_buffer[0]
    width, row_count = gradient.shape
    rank = warm_factor.shape[0]
    peers = replicas * groups
    chunk = row_count // peers
    norm_limit = 0.1 * math.sqrt(width * depth * groups * row_count)

    send = call(
        merge_kernel, shape((peers, width // 2, 2 * chunk + 128), BF16), gradient, error_buffer, warm_factor
    )
    got = lax.all_to_all(send, ("gx", "gz"), 0, 0)
    mean, send = call(
        lambda *refs: rows_kernel(groups, width, 1.0 / replicas, *refs),
        (shape((groups * width, chunk), F32), shape((depth, rank, chunk), BF16)),
        got,
    )
    got = lax.all_to_all(send, "gy", 0, 0)
    send = call(
        lambda *refs: columns_kernel(groups, *refs), shape((peers, rank, chunk + 128), BF16), got, mean
    )
    got = lax.all_to_all(send, ("gx", "gz"), 0, 0)
    rows, next_factor, mix, norm = call(
        factor_kernel,
        (
            shape((rank, row_count), BF16),
            shape((rank, width), F32),
            shape((width, 128), BF16),
            shape((depth * groups, 128), F32),
        ),
        got,
    )
    norms = lax.all_to_all(norm, ("gy", "gz"), 0, 0, tiled=True)
    applied, next_error = call(
        lambda *refs: update_kernel(norm_limit, *refs),
        (shape((width, row_count), BF16), shape((width, row_count), BF16)),
        norms,
        mix,
        rows,
        gradient,
        error_buffer,
    )
    return applied, next_error[None], next_factor


def solution(mesh):
    in_specs = (P("gx", ("gy", "gz"), None), P("gx", ("gy", "gz"), None), P(None, ("gy", "gz")))
    out_specs = (P(("gy", "gz"), None), P("gx", ("gy", "gz"), None), P(None, ("gy", "gz")))
    return jax.shard_map(
        per_device, mesh=mesh, in_specs=in_specs, out_specs=out_specs, check_vma=False
    )
```

time: 671 us -> 103 us (0.15)
  the two profiles are of different devices: /device:TPU:8 before, /device:TPU:1 now
where the time goes in v1:
time: 103 us; the launch traced here: 102 us
  blocking collectives  92.6 us (90%)
  Pallas kernels  6.06 us (6%)
  local copies, waits for them, and re-layouts  2.8 us (3%)
    all_to_all x2, blocking collectives, per_device(): got = lax.all_to_all(send, ('gx', 'gz'), 0, 0)  45.5 us
    all_to_all x1, blocking collectives, per_device(): got = lax.all_to_all(send, 'gy', 0, 0)  26.3 us
    all_to_all x1, blocking collectives, per_device(): norms = lax.all_to_all(norm, ('gy', 'gz'), 0, 0, tiled=True)  20.8 us
    pallas_call x5, Pallas kernels, call(): pl.pallas_call(kernel, out_shape=outs, in_specs=[pl.BlockSpec(memory_spac...  6.06 us
    unnamed x10, local copies, waits for them, and re-layouts  2.8 us

profile of v1, /device:TPU:1, one launch (start us, length us, event | category | flops | bytes accessed | tf_op | source)
XLA Modules:
  0.0 102.1 jit_solution(18239596949006609068)
XLA Ops:
  0.6 0.0 copy-start
  0.6 1.0 %copy-done = bf16[1,32,8192]{2,1,0:T(8,128)(2,1)S(1)} copy-done((bf16[1,32,8192]{2,1,0:T(8,128)(2,1)S(1)}, bf16[1,32,8192]{2,1,0:T(8,128)(2,1)}, u32[]{:S(2)}) %copy-start) | copy-done | bytes 524312
  1.7 0.0 copy-start.2
  1.7 1.0 %copy-done.2 = bf16[1,32,8192]{2,1,0:T(8,128)(2,1)S(1)} copy-done((bf16[1,32,8192]{2,1,0:T(8,128)(2,1)S(1)}, bf16[1,32,8192]{2,1,0:T(8,128)(2,1)}, u32[]{:S(2)}) %copy-start.2) | copy-done | bytes 524312
  2.7 0.0 copy-start.4
  2.7 0.7 copy-done.4
  3.4 0.1 shard_map.58
  3.6 21.9 %all_to_all.26.refs_0_ = bf16[32,16,640]{2,1,0:T(8,128)(2,1)S(1)} all-to-all(bf16[32,16,640]{2,1,0:T(8,128)(2,1)S(1)} %shard_map.58), channel_id=1, replica_groups=mesh['gx'=8,'gy'=16,'gz'=4] {'gx','gz'}, dimensions={0} | all-to-all | bytes 1310720 | tf_op jit(solution)/shard_map/all_to_all | solution.py:162
  25.4 0.3 shard_map.59
  25.7 26.3 %all_to_all.27.refs_0_ = bf16[16,32,256]{2,1,0:T(8,128)(2,1)S(1)} all-to-all(bf16[16,32,256]{2,1,0:T(8,128)(2,1)S(1)} %get-tuple-element.11), channel_id=1, replica_groups=mesh['gx'=8,'gy'=16,'gz'=4] {'gy'}, dimensions={0} | all-to-all | bytes 524288 | tf_op jit(solution)/shard_map/all_to_all | solution.py:168
  52.0 0.4 shard_map.60
  52.4 0.0 copy-start.3
  52.4 23.7 %all_to_all.28.got_ref = bf16[32,32,384]{2,1,0:T(8,128)(2,1)S(1)} all-to-all(bf16[32,32,384]{2,1,0:T(8,128)(2,1)S(1)} %shard_map.60), channel_id=1, replica_groups=mesh['gx'=8,'gy'=16,'gz'=4] {'gx','gz'}, dimensions={0} | all-to-all | bytes 1572864 | tf_op jit(solution)/shard_map/all_to_all | solution.py:172
  76.1 0.0 copy-start.1
  76.1 3.9 %shard_map.61 = (bf16[32,8192]{1,0:T(8,128)(2,1)S(1)}, f32[32,32]{1,0:T(8,128)}, bf16[32,128]{1,0:T(8,128)(2,1)S(1)}, f32[64,128]{1,0:T(8,128)S(1)}) custom-call(bf16[32,32,384]{2,1,0:T(8,128)(2,1)S(1)} %all_to_all.28.got_ref), custom_call_target="tpu_custom_call" | custom-call | tf_op jit(solution)/shard_map/pallas_call | solution.py:140
  80.0 20.8 %all_to_all.29 = f32[64,1,128]{2,1,0:T(1,128)S(1)} all-to-all(f32[64,1,128]{2,1,0:T(1,128)S(1)} %bitcast.12), channel_id=1, replica_groups=mesh['gx'=8,'gy'=16,'gz'=4] {'gy','gz'}, dimensions={0} | all-to-all | bytes 65536 | tf_op jit(solution)/shard_map/all_to_all | solution.py:183
  100.7 0.0 copy-done.3
  100.7 0.0 copy-done.1
  100.7 1.3 %shard_map.62 = (bf16[32,8192]{1,0:T(8,128)(2,1)}, bf16[32,8192]{1,0:T(8,128)(2,1)}) custom-call(f32[64,128]{1,0:T(8,128)S(1)} %bitcast.11, bf16[32,128]{1,0:T(8,128)(2,1)S(1)} %get-tuple-element.14.refs_1_, bf16[32,8192]{1,0:T(8,128)(2,1)S(1)} %get-tuple-element.15.refs_2_, bf16[32,8192]{1,0:T(8,128)(2,1)S(1)} %bitcast.8, bf16[32,8192]{1,0:T(8,128)(2,1)S(1)} %bitcast.10), custom_call_target="tpu_custom_call" | custom-call | tf_op jit(solution)/shard_map/pallas_call | solution.py:140
Async XLA Ops:
  0.6 1.0 %copy-start = (bf16[1,32,8192]{2,1,0:T(8,128)(2,1)S(1)}, bf16[1,32,8192]{2,1,0:T(8,128)(2,1)}, u32[]{:S(2)}) copy-start(bf16[1,32,8192]{2,1,0:T(8,128)(2,1)} %param.3) | copy-start | bytes 1572868
  1.7 1.0 %copy-start.2 = (bf16[1,32,8192]{2,1,0:T(8,128)(2,1)S(1)}, bf16[1,32,8192]{2,1,0:T(8,128)(2,1)}, u32[]{:S(2)}) copy-start(bf16[1,32,8192]{2,1,0:T(8,128)(2,1)} %param.4) | copy-start | bytes 1572868
  2.7 0.7 copy-start.4
  52.4 48.3 %copy-start.3 = (bf16[1,32,8192]{2,1,0:T(8,128)(2,1)S(1)}, bf16[1,32,8192]{2,1,0:T(8,128)(2,1)}, u32[]{:S(2)}) copy-start(bf16[1,32,8192]{2,1,0:T(8,128)(2,1)} %param.4) | copy-start | bytes 1572868
  76.1 24.7 %copy-start.1 = (bf16[1,32,8192]{2,1,0:T(8,128)(2,1)S(1)}, bf16[1,32,8192]{2,1,0:T(8,128)(2,1)}, u32[]{:S(2)}) copy-start(bf16[1,32,8192]{2,1,0:T(8,128)(2,1)} %param.3) | copy-start | bytes 1572868

commit v2 on v1

--- a/solution.py
+++ b/solution.py
@@ -13,25 +13,46 @@
 PARAMS = pltpu.CompilerParams(vmem_limit_bytes=16 * 1024 * 1024)
 
 
-def split3(value):
-    high = value.astype(BF16)
-    rest = value - high.astype(F32)
-    middle = rest.astype(BF16)
-    low = (rest - middle.astype(F32)).astype(BF16)
-    return high, middle, low
-
-
-def merge_kernel(gradient_ref, error_ref, warm_ref, send_ref):
+def split(value, pieces):
+    parts = []
+    for _ in range(pieces):
+        part = value.astype(BF16)
+        parts.append(part)
+        value = value - part.astype(F32)
+    return parts
+
+
+def merge_kernel(gradient_ref, error_ref, warm_ref, send_ref, gradient_tile, error_tile, warm_tile, sems):
     peers, half, _ = send_ref.shape
     chunk = gradient_ref.shape[1] // peers
     rank, width = warm_ref.shape
-    warm = warm_ref[...].astype(BF16)
+    pieces = sems.shape[0]
+    per_piece = peers // pieces
+    copies = []
+    for piece in range(pieces):
+        part = pl.ds(piece * per_piece * chunk, per_piece * chunk)
+        copies.append(
+            (
+                pltpu.make_async_copy(gradient_ref.at[:, part], gradient_tile.at[:, part], sems.at[piece, 0]),
+                pltpu.make_async_copy(error_ref.at[:, part], error_tile.at[:, part], sems.at[piece, 1]),
+            )
+        )
+    warm_copy = pltpu.make_async_copy(warm_ref, warm_tile, sems.at[0, 2])
+    warm_copy.start()
+    for pair in copies:
+        pair[0].start()
+        pair[1].start()
+    warm_copy.wait()
+    warm = warm_tile[...].astype(BF16)
     packed = jnp.concatenate(
         [warm[:half], warm[half:], jnp.zeros((half, 128 - 2 * width), BF16)], axis=1
     )
     for peer in range(peers):
+        if peer % per_piece == 0:
+            copies[peer // per_piece][0].wait()
+            copies[peer // per_piece][1].wait()
         part = slice(peer * chunk, (peer + 1) * chunk)
-        tile = (gradient_ref[:, part].astype(F32) + error_ref[:, part].astype(F32)).astype(BF16)
+        tile = (gradient_tile[:, part].astype(F32) + error_tile[:, part].astype(F32)).astype(BF16)
         send_ref[peer, :, 0:chunk] = tile[:half]
         send_ref[peer, :, chunk : 2 * chunk] = tile[half:]
         send_ref[peer, :, 2 * chunk :] = packed
@@ -59,12 +80,23 @@
         send_ref[peer] = rows
 
 
+def add(got_ref):
+    total = got_ref[0].astype(F32)
+    for peer in range(1, got_ref.shape[0]):
+        total += got_ref[peer].astype(F32)
+    return total.astype(BF16)
+
+
+def sum_kernel(got_ref, send_ref):
+    total = add(got_ref)
+    for peer in range(send_ref.shape[0]):
+        send_ref[peer] = total
+
+
 def columns_kernel(groups, got_ref, mean_ref, send_ref):
-    peers, rank, chunk = got_ref.shape
-    total = got_ref[0].astype(F32)
-    for peer in range(1, peers):
-        total += got_ref[peer].astype(F32)
-    rows = total.astype(BF16)
+    chunk = got_ref.shape[2]
+    half = send_ref.shape[1]
+    rows = add(got_ref)
     product = lax.dot_general(
         rows.astype(F32),
         mean_ref[...],
@@ -74,24 +106,28 @@
     )
     width = product.shape[1] // groups
     for group in range(groups):
-        pieces = split3(product[:, group * width : (group + 1) * width])
-        pad = jnp.zeros((rank, 128 - 3 * width), BF16)
-        tail = jnp.concatenate([*pieces, pad], axis=1)
+        high, low = split(product[:, group * width : (group + 1) * width], 2)
+        tail = jnp.concatenate([high[:half], high[half:], low[:half], low[half:]], axis=1)
         for replica in range(send_ref.shape[0] // groups):
-            send_ref[replica * groups + group, :, 0:chunk] = rows
-            send_ref[replica * groups + group, :, chunk:] = tail
+            peer = replica * groups + group
+            send_ref[peer, :, 0:chunk] = rows[:half]
+            send_ref[peer, :, chunk : 2 * chunk] = rows[half:]
+            send_ref[peer, :, 2 * chunk :] = tail
 
 
 def factor_kernel(got_ref, rows_ref, next_ref, mix_ref, norm_ref):
-    peers, rank, wide = got_ref.shape
-    chunk = wide - 128
-    width = next_ref.shape[1]
-    tails = got_ref[0, :, chunk:].astype(F32)
+    peers, half, wide = got_ref.shape
+    chunk = (wide - 128) // 2
+    rank, width = next_ref.shape
+    tails = got_ref[0, :, 2 * chunk :].astype(F32)
     for peer in range(1, peers):
-        tails += got_ref[peer, :, chunk:].astype(F32)
-    product = tails[:, :width] + tails[:, width : 2 * width] + tails[:, 2 * width : 3 * width]
+        tails += got_ref[peer, :, 2 * chunk :].astype(F32)
+    tails = tails[:, : 2 * width] + tails[:, 2 * width :]
+    product = jnp.concatenate([tails[:, :width], tails[:, width:]], axis=0)
     for peer in range(peers):
-        rows_ref[:, peer * chunk : (peer + 1) * chunk] = got_ref[peer, :, 0:chunk]
+        part = slice(peer * chunk, (peer + 1) * chunk)
+        rows_ref[0:half, part] = got_ref[peer, :, 0:chunk]
+        rows_ref[half:rank, part] = got_ref[peer, :, chunk : 2 * chunk]
     rows = rows_ref[...]
     gram = lax.dot_general(rows, rows, (((1,), (1,)), ((), ())), preferred_element_type=F32)
     line = lax.broadcasted_iota(jnp.int32, (rank, rank), 0)
@@ -116,7 +152,7 @@
         precision=HIGHEST,
         preferred_element_type=F32,
     )
-    mix_ref[...] = jnp.concatenate([*split3(mix), jnp.zeros((width, 128 - 3 * rank), BF16)], axis=1)
+    mix_ref[...] = jnp.concatenate([*split(mix, 3), jnp.zeros((width, 128 - 3 * rank), BF16)], axis=1)
 
 
 def update_kernel(norm_limit, norms_ref, mix_ref, rows_ref, gradient_ref, error_ref, applied_ref, next_ref):
@@ -136,19 +172,21 @@
         next_ref[:, part] = (tile.astype(F32) - decompressed).astype(BF16)
 
 
-def call(kernel, outs, *args):
+def call(kernel, outs, *args, space=pltpu.VMEM, scratch=()):
     return pl.pallas_call(
         kernel,
         out_shape=outs,
-        in_specs=[pl.BlockSpec(memory_space=pltpu.VMEM)] * len(args),
+        in_specs=[pl.BlockSpec(memory_space=space)] * len(args),
         out_specs=jax.tree.map(lambda _: pl.BlockSpec(memory_space=pltpu.VMEM), outs),
+        scratch_shapes=scratch,
         compiler_params=PARAMS,
     )(*args)
 
 
 def per_device(gradient, error_buffer, warm_factor):
     shape = jax.ShapeDtypeStruct
-    replicas, depth, groups = (lax.axis_size(axis) for axis in ("gx", "gy", "gz"))
+    replicas, far, near, groups = (lax.axis_size(axis) for axis in ("gx", "far", "near", "gz"))
+    depth = far * near
     gradient, error_buffer = gradient[0], error_buffer[0]
     width, row_count = gradient.shape
     rank = warm_factor.shape[0]
@@ -157,17 +195,33 @@
     norm_limit = 0.1 * math.sqrt(width * depth * groups * row_count)
 
     send = call(
-        merge_kernel, shape((peers, width // 2, 2 * chunk + 128), BF16), gradient, error_buffer, warm_factor
+        merge_kernel,
+        shape((peers, width // 2, 2 * chunk + 128), BF16),
+        gradient,
+        error_buffer,
+        warm_factor,
+        space=pl.ANY,
+        scratch=[
+            pltpu.VMEM((width, row_count), BF16),
+            pltpu.VMEM((width, row_count), BF16),
+            pltpu.VMEM((rank, width), F32),
+            pltpu.SemaphoreType.DMA((min(8, peers), 3)),
+        ],
     )
     got = lax.all_to_all(send, ("gx", "gz"), 0, 0)
     mean, send = call(
         lambda *refs: rows_kernel(groups, width, 1.0 / replicas, *refs),
-        (shape((groups * width, chunk), F32), shape((depth, rank, chunk), BF16)),
+        (shape((groups * width, chunk), F32), shape((far, rank, chunk), BF16)),
         got,
     )
-    got = lax.all_to_all(send, "gy", 0, 0)
+    got = lax.all_to_all(send, "far", 0, 0)
+    send = call(sum_kernel, shape((near, rank, chunk), BF16), got)
+    got = lax.all_to_all(send, "near", 0, 0)
     send = call(
-        lambda *refs: columns_kernel(groups, *refs), shape((peers, rank, chunk + 128), BF16), got, mean
+        lambda *refs: columns_kernel(groups, *refs),
+        shape((peers, rank // 2, 2 * chunk + 128), BF16),
+        got,
+        mean,
     )
     got = lax.all_to_all(send, ("gx", "gz"), 0, 0)
     rows, next_factor, mix, norm = call(
@@ -180,7 +234,7 @@
         ),
         got,
     )
-    norms = lax.all_to_all(norm, ("gy", "gz"), 0, 0, tiled=True)
+    norms = lax.all_to_all(norm, ("far", "near", "gz"), 0, 0, tiled=True)
     applied, next_error = call(
         lambda *refs: update_kernel(norm_limit, *refs),
         (shape((width, row_count), BF16), shape((width, row_count), BF16)),
@@ -194,8 +248,14 @@
 
 
 def solution(mesh):
-    in_specs = (P("gx", ("gy", "gz"), None), P("gx", ("gy", "gz"), None), P(None, ("gy", "gz")))
-    out_specs = (P(("gy", "gz"), None), P("gx", ("gy", "gz"), None), P(None, ("gy", "gz")))
+    replicas, depth, groups = (mesh.shape[axis] for axis in ("gx", "gy", "gz"))
+    near = max(n for n in range(1, depth + 1) if depth % n == 0 and n * n <= depth)
+    fine = jax.sharding.Mesh(
+        mesh.devices.reshape(replicas, depth // near, near, groups), ("gx", "far", "near", "gz")
+    )
+    columns = ("far", "near", "gz")
+    in_specs = (P("gx", columns, None), P("gx", columns, None), P(None, columns))
+    out_specs = (P(columns, None), P("gx", columns, None), P(None, columns))
     return jax.shard_map(
-        per_device, mesh=mesh, in_specs=in_specs, out_specs=out_specs, check_vma=False
-    )
+        per_device, mesh=fine, in_specs=in_specs, out_specs=out_specs, check_vma=False
+    )

time: 103 us -> 102 us (level)
    all_to_all x2, blocking collectives: 45.5 us -> 41.7 us  [per_device(): got = lax.all_to_all(send, ('gx', 'gz'), 0, 0)]
    all_to_all x2 -> x3, blocking collectives: 47 us -> 50.1 us  [the longest x1 25.1 us: per_device(): got = lax.all_to_all(send, 'far', 0, 0)]
    pallas_call x5 -> x6, Pallas kernels: 6.06 us -> 6.68 us  [call(): pl.pallas_call(kernel, out_shape=outs, in_specs=[pl.BlockSpec(memory_spac...]
where the time goes in v2:
time: 102 us
  blocking collectives  91.8 us (90%)
  Pallas kernels  6.68 us (7%)
  local copies, waits for them, and re-layouts  2.8 us (3%)
    all_to_all x2, blocking collectives, per_device(): got = lax.all_to_all(send, ('gx', 'gz'), 0, 0)  41.7 us
    all_to_all x1, blocking collectives, per_device(): got = lax.all_to_all(send, 'far', 0, 0)  25.1 us
    all_to_all x1, blocking collectives, per_device(): norms = lax.all_to_all(norm, ('far', 'near', 'gz'), 0, 0, tiled=True)  17.8 us
    all_to_all x1, blocking collectives, per_device(): got = lax.all_to_all(send, 'near', 0, 0)  7.31 us
    pallas_call x6, Pallas kernels, call(): pl.pallas_call(kernel, out_shape=outs, in_specs=[pl.BlockSpec(memory_spac...  6.68 us
    unnamed x10, local copies, waits for them, and re-layouts  2.8 us

profile of v2, /device:TPU:1, one launch (start us, length us, event | category | flops | bytes accessed | tf_op | source)
XLA Modules:
  0.0 102.0 jit_solution(15752004072121034617)
XLA Ops:
  0.6 0.0 copy-start
  0.6 1.0 %copy-done = bf16[1,32,8192]{2,1,0:T(8,128)(2,1)S(1)} copy-done((bf16[1,32,8192]{2,1,0:T(8,128)(2,1)S(1)}, bf16[1,32,8192]{2,1,0:T(8,128)(2,1)}, u32[]{:S(2)}) %copy-start) | copy-done | bytes 524312
  1.7 0.0 copy-start.2
  1.7 1.0 %copy-done.2 = bf16[1,32,8192]{2,1,0:T(8,128)(2,1)S(1)} copy-done((bf16[1,32,8192]{2,1,0:T(8,128)(2,1)S(1)}, bf16[1,32,8192]{2,1,0:T(8,128)(2,1)}, u32[]{:S(2)}) %copy-start.2) | copy-done | bytes 524312
  2.7 0.0 copy-start.4
  2.7 0.7 copy-done.4
  3.4 0.8 shard_map.58
  4.2 21.9 %all_to_all.31.refs_0_ = bf16[32,16,640]{2,1,0:T(8,128)(2,1)S(1)} all-to-all(bf16[32,16,640]{2,1,0:T(8,128)(2,1)S(1)} %shard_map.58), channel_id=1, replica_groups=mesh['gx'=8,'far'=4,'near'=4,'gz'=4] {'gx','gz'}, dimensions={0} | all-to-all | bytes 1310720 | tf_op jit(solution)/shard_map/all_to_all | solution.py:211
  26.1 0.3 shard_map.59
  26.4 25.1 %all_to_all.32.got_ref = bf16[4,32,256]{2,1,0:T(8,128)(2,1)S(1)} all-to-all(bf16[4,32,256]{2,1,0:T(8,128)(2,1)S(1)} %get-tuple-element.11), channel_id=1, replica_groups=mesh['gx'=8,'far'=4,'near'=4,'gz'=4] {'far'}, dimensions={0} | all-to-all | bytes 131072 | tf_op jit(solution)/shard_map/all_to_all | solution.py:217
  51.5 7.3 %all_to_all.33.refs_0_ = bf16[4,32,256]{2,1,0:T(8,128)(2,1)S(1)} all-to-all(bf16[4,32,256]{2,1,0:T(8,128)(2,1)S(1)} %shard_map.60), channel_id=1, replica_groups=mesh['gx'=8,'far'=4,'near'=4,'gz'=4] {'near'}, dimensions={0} | all-to-all | bytes 131072 | tf_op jit(solution)/shard_map/all_to_all | solution.py:219
  58.8 0.3 shard_map.61
  59.1 0.0 copy-start.3
  59.1 19.8 %all_to_all.34.got_ref = bf16[32,16,640]{2,1,0:T(8,128)(2,1)S(1)} all-to-all(bf16[32,16,640]{2,1,0:T(8,128)(2,1)S(1)} %shard_map.61), channel_id=1, replica_groups=mesh['gx'=8,'far'=4,'near'=4,'gz'=4] {'gx','gz'}, dimensions={0} | all-to-all | bytes 1310720 | tf_op jit(solution)/shard_map/all_to_all | solution.py:226
  79.0 0.0 copy-start.1
  79.0 3.9 %shard_map.62 = (bf16[32,8192]{1,0:T(8,128)(2,1)S(1)}, f32[32,32]{1,0:T(8,128)}, bf16[32,128]{1,0:T(8,128)(2,1)S(1)}, f32[64,128]{1,0:T(8,128)S(1)}) custom-call(bf16[32,16,640]{2,1,0:T(8,128)(2,1)S(1)} %all_to_all.34.got_ref), custom_call_target="tpu_custom_call" | custom-call | tf_op jit(solution)/shard_map/pallas_call | solution.py:176
  82.9 17.8 %all_to_all.35 = f32[64,1,128]{2,1,0:T(1,128)S(1)} all-to-all(f32[64,1,128]{2,1,0:T(1,128)S(1)} %bitcast.12), channel_id=1, replica_groups=mesh['gx'=8,'far'=4,'near'=4,'gz'=4] {'far','near','gz'}, dimensions={0} | all-to-all | bytes 65536 | tf_op jit(solution)/shard_map/all_to_all | solution.py:237
  100.6 0.0 copy-done.3
  100.6 0.0 copy-done.1
  100.6 1.4 %shard_map.63 = (bf16[32,8192]{1,0:T(8,128)(2,1)}, bf16[32,8192]{1,0:T(8,128)(2,1)}) custom-call(f32[64,128]{1,0:T(8,128)S(1)} %bitcast.11, bf16[32,128]{1,0:T(8,128)(2,1)S(1)} %get-tuple-element.14.refs_1_, bf16[32,8192]{1,0:T(8,128)(2,1)S(1)} %get-tuple-element.15.refs_2_, bf16[32,8192]{1,0:T(8,128)(2,1)S(1)} %bitcast.8, bf16[32,8192]{1,0:T(8,128)(2,1)S(1)} %bitcast.10), custom_call_target="tpu_custom_call" | custom-call | tf_op jit(solution)/shard_map/pallas_call | solution.py:176
  (1 shorter events, 0.0 us)
Async XLA Ops:
  0.6 1.0 %copy-start = (bf16[1,32,8192]{2,1,0:T(8,128)(2,1)S(1)}, bf16[1,32,8192]{2,1,0:T(8,128)(2,1)}, u32[]{:S(2)}) copy-start(bf16[1,32,8192]{2,1,0:T(8,128)(2,1)} %param.3) | copy-start | bytes 1572868
  1.7 1.0 %copy-start.2 = (bf16[1,32,8192]{2,1,0:T(8,128)(2,1)S(1)}, bf16[1,32,8192]{2,1,0:T(8,128)(2,1)}, u32[]{:S(2)}) copy-start(bf16[1,32,8192]{2,1,0:T(8,128)(2,1)} %param.4) | copy-start | bytes 1572868
  2.7 0.7 copy-start.4
  59.1 41.5 %copy-start.3 = (bf16[1,32,8192]{2,1,0:T(8,128)(2,1)S(1)}, bf16[1,32,8192]{2,1,0:T(8,128)(2,1)}, u32[]{:S(2)}) copy-start(bf16[1,32,8192]{2,1,0:T(8,128)(2,1)} %param.4) | copy-start | bytes 1572868
  79.0 21.7 %copy-start.1 = (bf16[1,32,8192]{2,1,0:T(8,128)(2,1)S(1)}, bf16[1,32,8192]{2,1,0:T(8,128)(2,1)}, u32[]{:S(2)}) copy-start(bf16[1,32,8192]{2,1,0:T(8,128)(2,1)} %param.3) | copy-start | bytes 1572868

commit v3 on v2

v3 whole, which is shorter than its diff:
```python
import math

import jax
import jax.numpy as jnp
from jax import lax
from jax.experimental import pallas as pl
from jax.experimental.pallas import tpu as pltpu
from jax.sharding import PartitionSpec as P

F32 = jnp.float32
BF16 = jnp.bfloat16
HIGHEST = lax.Precision.HIGHEST
LANES = 128


def split(value, pieces):
    parts = []
    for _ in range(pieces):
        part = value.astype(BF16)
        parts.append(part)
        value = value - part.astype(F32)
    return parts


def merge_kernel(
    gradient_ref, error_ref, warm_ref, send_ref, gradient_tile, error_tile, warm_tile, send_tile, got_sems, put_sems
):
    peers, tall, _ = send_ref.shape
    width, row_count = gradient_ref.shape
    chunk = row_count // peers
    rank = warm_ref.shape[0]
    pieces = put_sems.shape[0]
    per_piece = peers // pieces
    gets, puts = [], []
    for piece in range(pieces):
        part = pl.ds(piece * per_piece * chunk, per_piece * chunk)
        mine = pl.ds(piece * per_piece, per_piece)
        gets.append(
            (
                pltpu.make_async_copy(gradient_ref.at[:, part], gradient_tile.at[:, part], got_sems.at[piece, 0]),
                pltpu.make_async_copy(error_ref.at[:, part], error_tile.at[:, part], got_sems.at[piece, 1]),
            )
        )
        puts.append(pltpu.make_async_copy(send_tile.at[mine], send_ref.at[mine], put_sems.at[piece]))
    warm_get = pltpu.make_async_copy(warm_ref, warm_tile, got_sems.at[0, 2])
    warm_get.start()
    for pair in gets:
        pair[0].start()
        pair[1].start()
    warm_get.wait()
    half = rank // 2
    packed = jnp.concatenate(
        [warm_tile[:half], warm_tile[half:], jnp.zeros((half, LANES - 2 * width), F32)], axis=1
    ).astype(BF16)
    for piece in range(pieces):
        gets[piece][0].wait()
        gets[piece][1].wait()
        for peer in range(piece * per_piece, (piece + 1) * per_piece):
            for i in range(chunk // LANES):
                part = slice(peer * chunk + i * LANES, peer * chunk + (i + 1) * LANES)
                tile = gradient_tile[:, part].astype(F32) + error_tile[:, part].astype(F32)
                send_tile[peer, i * width : (i + 1) * width, :] = tile.astype(BF16)
            send_tile[peer, tall - half :, :] = packed
        puts[piece].start()
    for put in puts:
        put.wait()


def rows_kernel(groups, width, scale, got_ref, mean_ref, send_ref):
    peers, tall, _ = got_ref.shape
    chunk = mean_ref.shape[1]
    high = width * chunk // LANES
    replicas = peers // groups
    warm = []
    for group in range(groups):
        total = got_ref[group, 0:high, :].astype(F32)
        for replica in range(1, replicas):
            total += got_ref[replica * groups + group, 0:high, :].astype(F32)
        total *= scale
        for i in range(chunk // LANES):
            mean_ref[group * width : (group + 1) * width, i * LANES : (i + 1) * LANES] = total[
                i * width : (i + 1) * width
            ]
        packed = got_ref[group, high:, :].astype(F32)
        warm.append(jnp.concatenate([packed[:, :width], packed[:, width : 2 * width]], axis=0))
    rows = jnp.dot(
        jnp.concatenate(warm, axis=1), mean_ref[...], precision=HIGHEST, preferred_element_type=F32
    ).astype(BF16)
    for peer in range(send_ref.shape[0]):
        send_ref[peer] = rows


def add(got_ref):
    total = got_ref[0].astype(F32)
    for peer in range(1, got_ref.shape[0]):
        total += got_ref[peer].astype(F32)
    return total.astype(BF16)


def sum_kernel(got_ref, send_ref):
    total = add(got_ref)
    for peer in range(send_ref.shape[0]):
        send_ref[peer] = total


def columns_kernel(groups, got_ref, mean_ref, send_ref):
    rank, chunk = got_ref.shape[1:]
    half = rank // 2
    rows = add(got_ref)
    product = lax.dot_general(
        rows.astype(F32),
        mean_ref[...],
        (((1,), (1,)), ((), ())),
        precision=HIGHEST,
        preferred_element_type=F32,
    )
    width = product.shape[1] // groups
    for group in range(groups):
        high, low = split(product[:, group * width : (group + 1) * width], 2)
        tail = jnp.concatenate([high[:half], high[half:], low[:half], low[half:]], axis=1)
        for replica in range(send_ref.shape[0] // groups):
            peer = replica * groups + group
            for i in range(chunk // LANES):
                send_ref[peer, i * rank : (i + 1) * rank, :] = rows[:, i * LANES : (i + 1) * LANES]
            send_ref[peer, chunk // LANES * rank :, :] = tail


def eliminate(gram, product):
    rank, width = product.shape
    columns = [
        jnp.broadcast_to(gram[8 * (j // 8) :, j : j + 1], (rank - 8 * (j // 8), LANES))
        for j in range(rank)
    ]
    line = lax.broadcasted_iota(jnp.int32, (rank, LANES), 0)
    lane = lax.broadcasted_iota(jnp.int32, (rank, LANES), 1)
    work = jnp.concatenate([product, jnp.zeros((rank, LANES - width), F32)], axis=1)
    work = jnp.where(lane == line + width, 1.0, work)
    for k in range(rank):
        top = 8 * (k // 8)
        column = columns[k]
        inverse_root = lax.rsqrt(column[k - top : k - top + 1])
        column = column * inverse_root
        for j in range(k + 1, rank):
            first = 8 * (j // 8) - top
            columns[j] = columns[j] - column[first:] * column[j - top : j - top + 1]
        row = work[k : k + 1] * inverse_root
        rest = work[top:] - jnp.where(line[top:] > k, column, 0.0) * row
        rest = jnp.where(line[top:] == k, row, rest)
        work = jnp.concatenate([work[:top], rest], axis=0) if top else rest
    return work[:, width : width + rank], work[:, :width]


def factor_kernel(got_ref, next_ref, mix_ref, norm_ref):
    peers, tall, _ = got_ref.shape
    rank, width = next_ref.shape
    high = tall - rank // 2
    tails = got_ref[0, high:, :].astype(F32)
    for peer in range(1, peers):
        tails += got_ref[peer, high:, :].astype(F32)
    tails = tails[:, : 2 * width] + tails[:, 2 * width :]
    product = jnp.concatenate([tails[:, :width], tails[:, width:]], axis=0)
    gram = jnp.zeros((rank, rank), F32)
    for peer in range(peers):
        rows = jnp.concatenate(
            [got_ref[peer, i : i + rank, :] for i in range(0, high, rank)], axis=1
        )
        gram += lax.dot_general(rows, rows, (((1,), (1,)), ((), ())), preferred_element_type=F32)
    line = lax.broadcasted_iota(jnp.int32, (rank, rank), 0)
    eye = (line == lax.broadcasted_iota(jnp.int32, (rank, rank), 1)).astype(F32)
    trace = jnp.sum(gram * eye)
    inverse, next_factor = eliminate(gram + (0.0001 * trace / rank) * eye, product)
    next_ref[...] = next_factor
    norm_ref[...] = jnp.full(norm_ref.shape, jnp.sum(next_factor * next_factor), F32)
    mix = lax.dot_general(
        next_factor,
        inverse,
        (((0,), (0,)), ((), ())),
        precision=HIGHEST,
        preferred_element_type=F32,
    )
    mix_ref[...] = jnp.concatenate(
        [*split(mix, 3), jnp.zeros((width, LANES - 3 * rank), BF16)], axis=1
    )


def residual_kernel(got_ref, mix_ref, gradient_ref, error_ref, decompressed_ref, next_ref):
    peers, tall, _ = got_ref.shape
    rank = next_ref.shape[0]
    high = tall - rank // 2
    chunk = high // rank * LANES
    mix = mix_ref[...][:, : 3 * rank]
    for peer in range(peers):
        part = slice(peer * chunk, (peer + 1) * chunk)
        rows = jnp.concatenate(
            [got_ref[peer, i : i + rank, :] for i in range(0, high, rank)], axis=1
        )
        decompressed = jnp.dot(
            mix, jnp.concatenate([rows, rows, rows], axis=0), preferred_element_type=F32
        )
        decompressed_ref[:, part] = decompressed
        tile = (gradient_ref[:, part].astype(F32) + error_ref[:, part].astype(F32)).astype(BF16)
        next_ref[:, part] = (tile.astype(F32) - decompressed).astype(BF16)


def clip_kernel(norm_limit, norms_ref, decompressed_ref, applied_ref, tile, sems):
    norm_sq = jnp.sum(norms_ref[...][:, 0:1])
    clip_scale = jnp.minimum(1.0, norm_limit * lax.rsqrt(jnp.full((1, 1), norm_sq + 1e-06, F32)))
    pieces = sems.shape[0]
    step = applied_ref.shape[1] // pieces
    puts = []
    for piece in range(pieces):
        part = pl.ds(piece * step, step)
        tile[:, part] = (clip_scale * decompressed_ref[:, part]).astype(BF16)
        put = pltpu.make_async_copy(tile.at[:, part], applied_ref.at[:, part], sems.at[piece])
        put.start()
        puts.append(put)
    for put in puts:
        put.wait()


def call(kernel, outs, *args, vmem=16, spaces=None, out_space=pltpu.VMEM, scratch=(), cost=None):
    spaces = spaces or [pltpu.VMEM] * len(args)
    return pl.pallas_call(
        kernel,
        out_shape=outs,
        in_specs=[pl.BlockSpec(memory_space=space) for space in spaces],
        out_specs=jax.tree.map(lambda _: pl.BlockSpec(memory_space=out_space), outs),
        scratch_shapes=scratch,
        compiler_params=pltpu.CompilerParams(vmem_limit_bytes=vmem * 1024 * 1024),
        cost_estimate=cost,
    )(*args)


def per_device(gradient, error_buffer, warm_factor):
    shape = jax.ShapeDtypeStruct
    replicas, far, near, groups = (lax.axis_size(axis) for axis in ("gx", "far", "near", "gz"))
    plane, columns = ("gx", "gz"), far * near * groups
    gradient, error_buffer = gradient[0], error_buffer[0]
    width, row_count = gradient.shape
    rank = warm_factor.shape[0]
    peers = replicas * groups
    chunk = row_count // peers
    norm_limit = 0.1 * math.sqrt(width * columns * row_count)
    pieces = min(8, peers)
    message = shape((peers, width * chunk // LANES + rank // 2, LANES), BF16)

    send = call(
        merge_kernel,
        message,
        gradient,
        error_buffer,
        warm_factor,
        vmem=60,
        spaces=[pl.ANY] * 3,
        out_space=pl.ANY,
        scratch=[
            pltpu.VMEM((width, row_count), BF16),
            pltpu.VMEM((width, row_count), BF16),
            pltpu.VMEM((rank, width), F32),
            pltpu.VMEM(message.shape, BF16),
            pltpu.SemaphoreType.DMA((pieces, 3)),
            pltpu.SemaphoreType.DMA((pieces,)),
        ],
    )
    got = lax.all_to_all(send, plane, 0, 0)
    mean, send = call(
        lambda *refs: rows_kernel(groups, width, 1.0 / replicas, *refs),
        (shape((groups * width, chunk), F32), shape((far, rank, chunk), BF16)),
        got,
    )
    got = lax.all_to_all(send, "far", 0, 0)
    send = call(sum_kernel, shape((near, rank, chunk), BF16), got)
    got = lax.all_to_all(send, "near", 0, 0)
    message = shape((peers, rank * chunk // LANES + rank // 2, LANES), BF16)
    send = call(lambda *refs: columns_kernel(groups, *refs), message, got, mean)
    got = lax.all_to_all(send, plane, 0, 0)
    next_factor, mix, norm = call(
        factor_kernel,
        (shape((rank, width), F32), shape((width, LANES), BF16), shape((columns, LANES), F32)),
        got,
    )
    norms = lax.all_to_all(norm, ("far", "near", "gz"), 0, 0, tiled=True)
    decompressed, next_error = call(
        residual_kernel,
        (shape((width, row_count), F32), shape((width, row_count), BF16)),
        got,
        mix,
        gradient,
        error_buffer,
        cost=pl.CostEstimate(
            flops=6 * rank * width * row_count, bytes_accessed=10 * width * row_count, transcendentals=0
        ),
    )
    applied = call(
        lambda *refs: clip_kernel(norm_limit, *refs),
        shape((width, row_count), BF16),
        norms,
        decompressed,
        out_space=pl.ANY,
        scratch=[pltpu.VMEM((width, row_count), BF16), pltpu.SemaphoreType.DMA((8,))],
    )
    return applied, next_error[None], next_factor


def solution(mesh):
    replicas, depth, groups = (mesh.shape[axis] for axis in ("gx", "gy", "gz"))
    near = max(n for n in range(1, depth + 1) if depth % n == 0 and n * n <= depth)
    fine = jax.sharding.Mesh(
        mesh.devices.reshape(replicas, depth // near, near, groups), ("gx", "far", "near", "gz")
    )
    columns = ("far", "near", "gz")
    in_specs = (P("gx", columns, None), P("gx", columns, None), P(None, columns))
    out_specs = (P(columns, None), P("gx", columns, None), P(None, columns))
    return jax.shard_map(
        per_device, mesh=fine, in_specs=in_specs, out_specs=out_specs, check_vma=False
    )
```

time: 102 us -> 99.1 us (0.972)
  blocking collectives: 91.8 us -> 74.3 us
  waiting for transfers between devices: 0 us -> 12.4 us
  starting transfers between devices: 0 us -> 4.59 us
  local copies, waits for them, and re-layouts: 2.8 us -> 0.01 us
    all_to_all x3 -> x2, blocking collectives: 59.5 us -> 42.6 us  [per_device(): got = lax.all_to_all(send, plane, 0, 0)]
    all_to_all x0 -> x1, waiting for transfers between devices: none -> 12.4 us  [per_device(): norms = lax.all_to_all(norm, ('far', 'near', 'gz'), 0, 0, tiled=True)]
    all_to_all x0 -> x1, starting transfers between devices: none -> 4.59 us  [per_device(): norms = lax.all_to_all(norm, ('far', 'near', 'gz'), 0, 0, tiled=True)]
    unnamed x10 -> x4, local copies, waits for them, and re-layouts: 2.8 us -> 0.01 us
    pallas_call x6 -> x7, Pallas kernels: 6.68 us -> 6.72 us  [call(): pl.pallas_call(kernel, out_shape=outs, in_specs=[pl.BlockSpec(memory_spac...]
  transfers between devices with their start and end apart: 0 -> 1, of which waited for: 0 -> 1; matrix products, arithmetic and copies ran while one was open for 0% -> 0% of each run, Pallas kernels for 0% -> 1%
where the time goes in v3:
time: 99.1 us; the launch traced here: 98.7 us
  blocking collectives  74.3 us (75%)
  waiting for transfers between devices  12.4 us (13%)
  Pallas kernels  6.72 us (7%)
  starting transfers between devices  4.59 us (5%)
    all_to_all x2, blocking collectives, per_device(): got = lax.all_to_all(send, plane, 0, 0)  42.6 us
    all_to_all x1, blocking collectives, per_device(): got = lax.all_to_all(send, 'far', 0, 0)  24.4 us
    all_to_all x1, waiting for transfers between devices, per_device(): norms = lax.all_to_all(norm, ('far', 'near', 'gz'), 0, 0, tiled=True)  12.4 us
    all_to_all x1, blocking collectives, per_device(): got = lax.all_to_all(send, 'near', 0, 0)  7.31 us
    pallas_call x7, Pallas kernels, call(): pl.pallas_call(kernel, out_shape=outs, in_specs=[pl.BlockSpec(memory_spac...  6.72 us
    all_to_all x1, starting transfers between devices, per_device(): norms = lax.all_to_all(norm, ('far', 'near', 'gz'), 0, 0, tiled=True)  4.59 us
  transfers between devices with their start and end apart: 1, of which 1 were waited for; matrix products, arithmetic and copies ran while one was open for 0% of the time, Pallas kernels for 1%

profile of v3, /device:TPU:1, one launch (start us, length us, event | category | flops | bytes accessed | tf_op | source)
XLA Modules:
  0.0 98.7 jit_solution(14589369539968558374)
XLA Ops:
  0.6 2.2 %shard_map.58 = bf16[32,80,128]{2,1,0:T(8,128)(2,1)} custom-call(bf16[32,8192]{1,0:T(8,128)(2,1)} %bitcast.7, bf16[32,8192]{1,0:T(8,128)(2,1)} %bitcast.9, f32[32,32]{1,0:T(8,128)} %warm_ref.1), custom_call_target="tpu_custom_call" | custom-call | tf_op jit(solution)/shard_map/pallas_call | solution.py:223
  2.8 22.8 %all_to_all.31.refs_0_ = bf16[32,80,128]{2,1,0:T(8,128)(2,1)S(1)} all-to-all(bf16[32,80,128]{2,1,0:T(8,128)(2,1)} %shard_map.58), channel_id=1, replica_groups=mesh['gx'=8,'far'=4,'near'=4,'gz'=4] {'gx','gz'}, dimensions={0} | all-to-all | bytes 1310720 | tf_op jit(solution)/shard_map/all_to_all | solution.py:265
  25.6 0.3 shard_map.59
  25.9 24.4 %all_to_all.32.got_ref = bf16[4,32,256]{2,1,0:T(8,128)(2,1)S(1)} all-to-all(bf16[4,32,256]{2,1,0:T(8,128)(2,1)S(1)} %get-tuple-element.10), channel_id=1, replica_groups=mesh['gx'=8,'far'=4,'near'=4,'gz'=4] {'far'}, dimensions={0} | all-to-all | bytes 131072 | tf_op jit(solution)/shard_map/all_to_all | solution.py:271
  50.3 7.3 %all_to_all.33.refs_0_ = bf16[4,32,256]{2,1,0:T(8,128)(2,1)S(1)} all-to-all(bf16[4,32,256]{2,1,0:T(8,128)(2,1)S(1)} %shard_map.60), channel_id=1, replica_groups=mesh['gx'=8,'far'=4,'near'=4,'gz'=4] {'near'}, dimensions={0} | all-to-all | bytes 131072 | tf_op jit(solution)/shard_map/all_to_all | solution.py:273
  57.6 0.3 shard_map.61
  57.9 0.0 copy-start.1
  57.9 19.8 %all_to_all.34.got_ref = bf16[32,80,128]{2,1,0:T(8,128)(2,1)S(1)} all-to-all(bf16[32,80,128]{2,1,0:T(8,128)(2,1)S(1)} %shard_map.61), channel_id=1, replica_groups=mesh['gx'=8,'far'=4,'near'=4,'gz'=4] {'gx','gz'}, dimensions={0} | all-to-all | bytes 1310720 | tf_op jit(solution)/shard_map/all_to_all | solution.py:276
  77.8 0.0 copy-start
  77.8 1.8 %shard_map.62 = (f32[32,32]{1,0:T(8,128)}, bf16[32,128]{1,0:T(8,128)(2,1)S(1)}, f32[64,128]{1,0:T(8,128)}) custom-call(bf16[32,80,128]{2,1,0:T(8,128)(2,1)S(1)} %all_to_all.34.got_ref), custom_call_target="tpu_custom_call" | custom-call | tf_op jit(solution)/shard_map/pallas_call | solution.py:223
  79.5 4.6 %all-to-all-start.4 = ((f32[64,1,128]{2,1,0:T(1,128)}), f32[64,1,128]{2,1,0:T(1,128)S(1)}, u32[]{:S(2)}, u32[]{:S(2)}) async-start(f32[64,1,128]{2,1,0:T(1,128)} %bitcast.3), calls=%async_computation.4 | async-start | bytes 65536 | tf_op jit(solution)/shard_map/all_to_all | solution.py:282
  84.1 0.0 copy-done.1
  84.1 0.0 copy-done
  84.1 1.1 %shard_map.63 = (f32[32,8192]{1,0:T(8,128)S(1)}, bf16[32,8192]{1,0:T(8,128)(2,1)}) custom-call(bf16[32,80,128]{2,1,0:T(8,128)(2,1)S(1)} %all_to_all.34.got_ref, bf16[32,128]{1,0:T(8,128)(2,1)S(1)} %get-tuple-element.13.mix_ref, bf16[32,8192]{1,0:T(8,128)(2,1)S(1)} %bitcast.8, bf16[32,8192]{1,0:T(8,128)(2,1)S(1)} %bitcast.10), custom_call_target="tpu_custom_call" | custom-call | flops 50331648 | bytes 2621440 | tf_op jit(solution)/shard_map/pallas_call | solution.py:223
  85.3 12.4 %all-to-all-done.4 = f32[64,1,128]{2,1,0:T(1,128)S(1)} async-done(((f32[64,1,128]{2,1,0:T(1,128)}), f32[64,1,128]{2,1,0:T(1,128)S(1)}, u32[]{:S(2)}, u32[]{:S(2)}) %all-to-all-start.4) | async-done | bytes 32800 | tf_op jit(solution)/shard_map/all_to_all | solution.py:282
  97.7 1.0 %shard_map.64 = bf16[32,8192]{1,0:T(8,128)(2,1)} custom-call(f32[64,128]{1,0:T(8,128)S(1)} %bitcast.11, f32[32,8192]{1,0:T(8,128)S(1)} %get-tuple-element.14.refs_1_), custom_call_target="tpu_custom_call" | custom-call | tf_op jit(solution)/shard_map/pallas_call | solution.py:223
  (1 shorter events, 0.0 us)
Async XLA Ops:
  57.9 26.2 %copy-start.1 = (bf16[1,32,8192]{2,1,0:T(8,128)(2,1)S(1)}, bf16[1,32,8192]{2,1,0:T(8,128)(2,1)}, u32[]{:S(2)}) copy-start(bf16[1,32,8192]{2,1,0:T(8,128)(2,1)} %param.4) | copy-start | bytes 1572868
  77.8 6.4 %copy-start = (bf16[1,32,8192]{2,1,0:T(8,128)(2,1)S(1)}, bf16[1,32,8192]{2,1,0:T(8,128)(2,1)}, u32[]{:S(2)}) copy-start(bf16[1,32,8192]{2,1,0:T(8,128)(2,1)} %param.3) | copy-start | bytes 1572868
  79.5 18.2 %all-to-all-start.4 = ((f32[64,1,128]{2,1,0:T(1,128)}), f32[64,1,128]{2,1,0:T(1,128)S(1)}, u32[]{:S(2)}, u32[]{:S(2)}) async-start(f32[64,1,128]{2,1,0:T(1,128)} %bitcast.3), calls=%async_computation.4 | async-start | bytes 65536 | tf_op jit(solution)/shard_map/all_to_all | solution.py:282

commit v4 on v3

--- a/solution.py
+++ b/solution.py
@@ -97,12 +97,6 @@
     return total.astype(BF16)
 
 
-def sum_kernel(got_ref, send_ref):
-    total = add(got_ref)
-    for peer in range(send_ref.shape[0]):
-        send_ref[peer] = total
-
-
 def columns_kernel(groups, got_ref, mean_ref, send_ref):
     rank, chunk = got_ref.shape[1:]
     half = rank // 2
@@ -234,7 +228,7 @@
 def per_device(gradient, error_buffer, warm_factor):
     shape = jax.ShapeDtypeStruct
     replicas, far, near, groups = (lax.axis_size(axis) for axis in ("gx", "far", "near", "gz"))
-    plane, columns = ("gx", "gz"), far * near * groups
+    plane, groups, columns = ("gx", "near", "gz"), near * groups, far * near * groups
     gradient, error_buffer = gradient[0], error_buffer[0]
     width, row_count = gradient.shape
     rank = warm_factor.shape[0]
@@ -269,8 +263,6 @@
         got,
     )
     got = lax.all_to_all(send, "far", 0, 0)
-    send = call(sum_kernel, shape((near, rank, chunk), BF16), got)
-    got = lax.all_to_all(send, "near", 0, 0)
     message = shape((peers, rank * chunk // LANES + rank // 2, LANES), BF16)
     send = call(lambda *refs: columns_kernel(groups, *refs), message, got, mean)
     got = lax.all_to_all(send, plane, 0, 0)
@@ -304,7 +296,7 @@
 
 def solution(mesh):
     replicas, depth, groups = (mesh.shape[axis] for axis in ("gx", "gy", "gz"))
-    near = max(n for n in range(1, depth + 1) if depth % n == 0 and n * n <= depth)
+    near = math.gcd(depth, 2)
     fine = jax.sharding.Mesh(
         mesh.devices.reshape(replicas, depth // near, near, groups), ("gx", "far", "near", "gz")
     )

time: 99.1 us -> 97.5 us (0.984)
  blocking collectives: 74.3 us -> 72.7 us
    all_to_all x1 -> x0, blocking collectives: 7.31 us -> none  [per_device(): got = lax.all_to_all(send, 'near', 0, 0)]
    all_to_all x2, blocking collectives: 42.6 us -> 47.8 us  [per_device(): got = lax.all_to_all(send, plane, 0, 0)]
    pallas_call x7 -> x6, Pallas kernels: 6.72 us -> 7.04 us  [call(): pl.pallas_call(kernel, out_shape=outs, in_specs=[pl.BlockSpec(memory_spac...]
where the time goes in v4:
time: 97.5 us; the launch traced here: 97.1 us
  blocking collectives  72.7 us (75%)
  waiting for transfers between devices  12.1 us (12%)
  Pallas kernels  7.04 us (7%)
  starting transfers between devices  4.59 us (5%)
    all_to_all x2, blocking collectives, per_device(): got = lax.all_to_all(send, plane, 0, 0)  47.8 us
    all_to_all x1, blocking collectives, per_device(): got = lax.all_to_all(send, 'far', 0, 0)  24.9 us
    all_to_all x1, waiting for transfers between devices, per_device(): norms = lax.all_to_all(norm, ('far', 'near', 'gz'), 0, 0, tiled=True)  12.1 us
    pallas_call x6, Pallas kernels, call(): pl.pallas_call(kernel, out_shape=outs, in_specs=[pl.BlockSpec(memory_spac...  7.04 us
    all_to_all x1, starting transfers between devices, per_device(): norms = lax.all_to_all(norm, ('far', 'near', 'gz'), 0, 0, tiled=True)  4.59 us
  transfers between devices with their start and end apart: 1, of which 1 were waited for; matrix products, arithmetic and copies ran while one was open for 0% of the time, Pallas kernels for 1%

profile of v4, /device:TPU:1, one launch (start us, length us, event | category | flops | bytes accessed | tf_op | source)
XLA Modules:
  0.0 97.1 jit_solution(9102161543719734405)
XLA Ops:
  0.6 2.2 %shard_map.58 = bf16[64,48,128]{2,1,0:T(8,128)(2,1)} custom-call(bf16[32,8192]{1,0:T(8,128)(2,1)} %bitcast.7, bf16[32,8192]{1,0:T(8,128)(2,1)} %bitcast.9, f32[32,32]{1,0:T(8,128)} %warm_ref.1), custom_call_target="tpu_custom_call" | custom-call | tf_op jit(solution)/shard_map/pallas_call | solution.py:217
  2.8 26.3 %all_to_all.26.refs_0_ = bf16[64,48,128]{2,1,0:T(8,128)(2,1)S(1)} all-to-all(bf16[64,48,128]{2,1,0:T(8,128)(2,1)} %shard_map.58), channel_id=1, replica_groups=mesh['gx'=8,'far'=8,'near'=2,'gz'=4] {'gx','near','gz'}, dimensions={0} | all-to-all | bytes 1572864 | tf_op jit(solution)/shard_map/all_to_all | solution.py:259
  29.2 0.3 shard_map.59
  29.5 24.9 %all_to_all.27.refs_0_ = bf16[8,32,128]{2,1,0:T(8,128)(2,1)S(1)} all-to-all(bf16[8,32,128]{2,1,0:T(8,128)(2,1)S(1)} %get-tuple-element.10), channel_id=1, replica_groups=mesh['gx'=8,'far'=8,'near'=2,'gz'=4] {'far'}, dimensions={0} | all-to-all | bytes 131072 | tf_op jit(solution)/shard_map/all_to_all | solution.py:265
  54.4 0.4 shard_map.60
  54.7 0.0 copy-start.1
  54.7 21.5 %all_to_all.28.got_ref = bf16[64,48,128]{2,1,0:T(8,128)(2,1)S(1)} all-to-all(bf16[64,48,128]{2,1,0:T(8,128)(2,1)S(1)} %shard_map.60), channel_id=1, replica_groups=mesh['gx'=8,'far'=8,'near'=2,'gz'=4] {'gx','near','gz'}, dimensions={0} | all-to-all | bytes 1572864 | tf_op jit(solution)/shard_map/all_to_all | solution.py:268
  76.3 0.0 copy-start
  76.3 1.9 %shard_map.61 = (f32[32,32]{1,0:T(8,128)}, bf16[32,128]{1,0:T(8,128)(2,1)S(1)}, f32[64,128]{1,0:T(8,128)}) custom-call(bf16[64,48,128]{2,1,0:T(8,128)(2,1)S(1)} %all_to_all.28.got_ref), custom_call_target="tpu_custom_call" | custom-call | tf_op jit(solution)/shard_map/pallas_call | solution.py:217
  78.1 4.6 %all-to-all-start.3 = ((f32[64,1,128]{2,1,0:T(1,128)}), f32[64,1,128]{2,1,0:T(1,128)S(1)}, u32[]{:S(2)}, u32[]{:S(2)}) async-start(f32[64,1,128]{2,1,0:T(1,128)} %bitcast.3), calls=%async_computation.3 | async-start | bytes 65536 | tf_op jit(solution)/shard_map/all_to_all | solution.py:274
  82.7 0.0 copy-done.1
  82.7 0.0 copy-done
  82.7 1.3 %shard_map.62 = (f32[32,8192]{1,0:T(8,128)S(1)}, bf16[32,8192]{1,0:T(8,128)(2,1)}) custom-call(bf16[64,48,128]{2,1,0:T(8,128)(2,1)S(1)} %all_to_all.28.got_ref, bf16[32,128]{1,0:T(8,128)(2,1)S(1)} %get-tuple-element.13.mix_ref, bf16[32,8192]{1,0:T(8,128)(2,1)S(1)} %bitcast.8, bf16[32,8192]{1,0:T(8,128)(2,1)S(1)} %bitcast.10), custom_call_target="tpu_custom_call" | custom-call | flops 50331648 | bytes 2621440 | tf_op jit(solution)/shard_map/pallas_call | solution.py:217
  84.1 12.1 %all-to-all-done.3 = f32[64,1,128]{2,1,0:T(1,128)S(1)} async-done(((f32[64,1,128]{2,1,0:T(1,128)}), f32[64,1,128]{2,1,0:T(1,128)S(1)}, u32[]{:S(2)}, u32[]{:S(2)}) %all-to-all-start.3) | async-done | bytes 32800 | tf_op jit(solution)/shard_map/all_to_all | solution.py:274
  96.1 1.0 %shard_map.63 = bf16[32,8192]{1,0:T(8,128)(2,1)} custom-call(f32[64,128]{1,0:T(8,128)S(1)} %bitcast.11, f32[32,8192]{1,0:T(8,128)S(1)} %get-tuple-element.14.refs_1_), custom_call_target="tpu_custom_call" | custom-call | tf_op jit(solution)/shard_map/pallas_call | solution.py:217
Async XLA Ops:
  54.7 28.0 %copy-start.1 = (bf16[1,32,8192]{2,1,0:T(8,128)(2,1)S(1)}, bf16[1,32,8192]{2,1,0:T(8,128)(2,1)}, u32[]{:S(2)}) copy-start(bf16[1,32,8192]{2,1,0:T(8,128)(2,1)} %param.4) | copy-start | bytes 1572868
  76.3 6.5 %copy-start = (bf16[1,32,8192]{2,1,0:T(8,128)(2,1)S(1)}, bf16[1,32,8192]{2,1,0:T(8,128)(2,1)}, u32[]{:S(2)}) copy-start(bf16[1,32,8192]{2,1,0:T(8,128)(2,1)} %param.3) | copy-start | bytes 1572868
  78.1 18.0 %all-to-all-start.3 = ((f32[64,1,128]{2,1,0:T(1,128)}), f32[64,1,128]{2,1,0:T(1,128)S(1)}, u32[]{:S(2)}, u32[]{:S(2)}) async-start(f32[64,1,128]{2,1,0:T(1,128)} %bitcast.3), calls=%async_computation.3 | async-start | bytes 65536 | tf_op jit(solution)/shard_map/all_to_all | solution.py:274

commit v5 on v4

--- a/solution.py
+++ b/solution.py
@@ -22,35 +22,31 @@
     return parts
 
 
-def merge_kernel(
-    gradient_ref, error_ref, warm_ref, send_ref, gradient_tile, error_tile, warm_tile, send_tile, got_sems, put_sems
-):
+def merge_kernel(gradient_ref, error_ref, warm_ref, send_ref, gradient_tile, error_tile, warm_tile, sems):
     peers, tall, _ = send_ref.shape
     width, row_count = gradient_ref.shape
     chunk = row_count // peers
     rank = warm_ref.shape[0]
-    pieces = put_sems.shape[0]
+    extra = rank * width // LANES
+    pieces = sems.shape[0]
     per_piece = peers // pieces
-    gets, puts = [], []
+    gets = []
     for piece in range(pieces):
         part = pl.ds(piece * per_piece * chunk, per_piece * chunk)
-        mine = pl.ds(piece * per_piece, per_piece)
         gets.append(
             (
-                pltpu.make_async_copy(gradient_ref.at[:, part], gradient_tile.at[:, part], got_sems.at[piece, 0]),
-                pltpu.make_async_copy(error_ref.at[:, part], error_tile.at[:, part], got_sems.at[piece, 1]),
+                pltpu.make_async_copy(gradient_ref.at[:, part], gradient_tile.at[:, part], sems.at[piece, 0]),
+                pltpu.make_async_copy(error_ref.at[:, part], error_tile.at[:, part], sems.at[piece, 1]),
             )
         )
-        puts.append(pltpu.make_async_copy(send_tile.at[mine], send_ref.at[mine], put_sems.at[piece]))
-    warm_get = pltpu.make_async_copy(warm_ref, warm_tile, got_sems.at[0, 2])
+    warm_get = pltpu.make_async_copy(warm_ref, warm_tile, sems.at[0, 2])
     warm_get.start()
     for pair in gets:
         pair[0].start()
         pair[1].start()
     warm_get.wait()
-    half = rank // 2
     packed = jnp.concatenate(
-        [warm_tile[:half], warm_tile[half:], jnp.zeros((half, LANES - 2 * width), F32)], axis=1
+        [warm_tile[i : i + extra] for i in range(0, rank, extra)], axis=1
     ).astype(BF16)
     for piece in range(pieces):
         gets[piece][0].wait()
@@ -59,11 +55,8 @@
             for i in range(chunk // LANES):
                 part = slice(peer * chunk + i * LANES, peer * chunk + (i + 1) * LANES)
                 tile = gradient_tile[:, part].astype(F32) + error_tile[:, part].astype(F32)
-                send_tile[peer, i * width : (i + 1) * width, :] = tile.astype(BF16)
-            send_tile[peer, tall - half :, :] = packed
-        puts[piece].start()
-    for put in puts:
-        put.wait()
+                send_ref[peer, i * width : (i + 1) * width, :] = tile.astype(BF16)
+            send_ref[peer, tall - extra :, :] = packed
 
 
 def rows_kernel(groups, width, scale, got_ref, mean_ref, send_ref):
@@ -82,7 +75,9 @@
                 i * width : (i + 1) * width
             ]
         packed = got_ref[group, high:, :].astype(F32)
-        warm.append(jnp.concatenate([packed[:, :width], packed[:, width : 2 * width]], axis=0))
+        warm.append(
+            jnp.concatenate([packed[:, i : i + width] for i in range(0, LANES, width)], axis=0)
+        )
     rows = jnp.dot(
         jnp.concatenate(warm, axis=1), mean_ref[...], precision=HIGHEST, preferred_element_type=F32
     ).astype(BF16)
@@ -144,19 +139,24 @@
     return work[:, width : width + rank], work[:, :width]
 
 
-def factor_kernel(got_ref, next_ref, mix_ref, norm_ref):
+def factor_kernel(got_ref, next_ref, pair_ref, norm_ref):
     peers, tall, _ = got_ref.shape
     rank, width = next_ref.shape
     high = tall - rank // 2
-    tails = got_ref[0, high:, :].astype(F32)
-    for peer in range(1, peers):
-        tails += got_ref[peer, high:, :].astype(F32)
-    tails = tails[:, : 2 * width] + tails[:, 2 * width :]
+    tails = [got_ref[peer, high:, :].astype(F32) for peer in range(peers)]
+    while len(tails) > 1:
+        tails = [sum(tails[i + 1 : i + 2], tails[i]) for i in range(0, len(tails), 2)]
+    tails = tails[0][:, : 2 * width] + tails[0][:, 2 * width :]
     product = jnp.concatenate([tails[:, :width], tails[:, width:]], axis=0)
     gram = jnp.zeros((rank, rank), F32)
-    for peer in range(peers):
+    for first in range(0, peers, 8):
         rows = jnp.concatenate(
-            [got_ref[peer, i : i + rank, :] for i in range(0, high, rank)], axis=1
+            [
+                got_ref[peer, i : i + rank, :]
+                for peer in range(first, min(first + 8, peers))
+                for i in range(0, high, rank)
+            ],
+            axis=1,
         )
         gram += lax.dot_general(rows, rows, (((1,), (1,)), ((), ())), preferred_element_type=F32)
     line = lax.broadcasted_iota(jnp.int32, (rank, rank), 0)
@@ -165,24 +165,25 @@
     inverse, next_factor = eliminate(gram + (0.0001 * trace / rank) * eye, product)
     next_ref[...] = next_factor
     norm_ref[...] = jnp.full(norm_ref.shape, jnp.sum(next_factor * next_factor), F32)
+    pair_ref[...] = jnp.concatenate(
+        [next_factor, inverse, jnp.zeros((rank, LANES - width - rank), F32)], axis=1
+    )
+
+
+def residual_kernel(got_ref, pair_ref, gradient_ref, error_ref, decompressed_ref, next_ref):
+    peers, tall, _ = got_ref.shape
+    rank = pair_ref.shape[0]
+    high = tall - rank // 2
+    chunk = high // rank * LANES
+    width = next_ref.shape[0]
     mix = lax.dot_general(
-        next_factor,
-        inverse,
+        pair_ref[:, :width],
+        pair_ref[:, width : width + rank],
         (((0,), (0,)), ((), ())),
         precision=HIGHEST,
         preferred_element_type=F32,
     )
-    mix_ref[...] = jnp.concatenate(
-        [*split(mix, 3), jnp.zeros((width, LANES - 3 * rank), BF16)], axis=1
-    )
-
-
-def residual_kernel(got_ref, mix_ref, gradient_ref, error_ref, decompressed_ref, next_ref):
-    peers, tall, _ = got_ref.shape
-    rank = next_ref.shape[0]
-    high = tall - rank // 2
-    chunk = high // rank * LANES
-    mix = mix_ref[...][:, : 3 * rank]
+    mix = jnp.concatenate(split(mix, 3), axis=1)
     for peer in range(peers):
         part = slice(peer * chunk, (peer + 1) * chunk)
         rows = jnp.concatenate(
@@ -235,25 +236,22 @@
     peers = replicas * groups
     chunk = row_count // peers
     norm_limit = 0.1 * math.sqrt(width * columns * row_count)
-    pieces = min(8, peers)
-    message = shape((peers, width * chunk // LANES + rank // 2, LANES), BF16)
+    pieces = min(4, peers)
+    message = shape((peers, (width * chunk + rank * width) // LANES, LANES), BF16)
 
     send = call(
         merge_kernel,
         message,
-        gradient,
-        error_buffer,
-        warm_factor,
-        vmem=60,
-        spaces=[pl.ANY] * 3,
-        out_space=pl.ANY,
+        *(
+            pltpu.with_memory_space_constraint(x, pltpu.HBM)
+            for x in (gradient, error_buffer, warm_factor)
+        ),
+        spaces=[pltpu.HBM] * 3,
         scratch=[
             pltpu.VMEM((width, row_count), BF16),
             pltpu.VMEM((width, row_count), BF16),
             pltpu.VMEM((rank, width), F32),
-            pltpu.VMEM(message.shape, BF16),
             pltpu.SemaphoreType.DMA((pieces, 3)),
-            pltpu.SemaphoreType.DMA((pieces,)),
         ],
     )
     got = lax.all_to_all(send, plane, 0, 0)
@@ -266,9 +264,9 @@
     message = shape((peers, rank * chunk // LANES + rank // 2, LANES), BF16)
     send = call(lambda *refs: columns_kernel(groups, *refs), message, got, mean)
     got = lax.all_to_all(send, plane, 0, 0)
-    next_factor, mix, norm = call(
+    next_factor, pair, norm = call(
         factor_kernel,
-        (shape((rank, width), F32), shape((width, LANES), BF16), shape((columns, LANES), F32)),
+        (shape((rank, width), F32), shape((rank, LANES), F32), shape((columns, LANES), F32)),
         got,
     )
     norms = lax.all_to_all(norm, ("far", "near", "gz"), 0, 0, tiled=True)
@@ -276,7 +274,7 @@
         residual_kernel,
         (shape((width, row_count), F32), shape((width, row_count), BF16)),
         got,
-        mix,
+        pair,
         gradient,
         error_buffer,
         cost=pl.CostEstimate(

time: 97.5 us -> 95 us (0.974)
  blocking collectives: 72.7 us -> 71.2 us
    all_to_all x2, blocking collectives: 47.8 us -> 45.6 us  [per_device(): got = lax.all_to_all(send, plane, 0, 0)]
  transfers between devices with their start and end apart: 1 -> 1, of which waited for: 1 -> 1; matrix products, arithmetic and copies ran while one was open for 0% -> 0% of each run, Pallas kernels for 1% -> 2%
where the time goes in v5:
time: 95 us; the launch traced here: 94.7 us
  blocking collectives  71.2 us (75%)
  waiting for transfers between devices  11.8 us (12%)
  Pallas kernels  6.49 us (7%)
  starting transfers between devices  4.59 us (5%)
    all_to_all x2, blocking collectives, per_device(): got = lax.all_to_all(send, plane, 0, 0)  45.6 us
    all_to_all x1, blocking collectives, per_device(): got = lax.all_to_all(send, 'far', 0, 0)  25.6 us
    all_to_all x1, waiting for transfers between devices, per_device(): norms = lax.all_to_all(norm, ('far', 'near', 'gz'), 0, 0, tiled=True)  11.8 us
    pallas_call x6, Pallas kernels, call(): pl.pallas_call(kernel, out_shape=outs, in_specs=[pl.BlockSpec(memory_spac...  6.49 us
    all_to_all x1, starting transfers between devices, per_device(): norms = lax.all_to_all(norm, ('far', 'near', 'gz'), 0, 0, tiled=True)  4.59 us
  transfers between devices with their start and end apart: 1, of which 1 were waited for; matrix products, arithmetic and copies ran while one was open for 0% of the time, Pallas kernels for 2%

profile of v5, /device:TPU:1, one launch (start us, length us, event | category | flops | bytes accessed | tf_op | source)
XLA Modules:
  0.0 94.7 jit_solution(11609958019865175200)
XLA Ops:
  0.6 1.4 %shard_map.58 = bf16[64,40,128]{2,1,0:T(8,128)(2,1)S(1)} custom-call(bf16[32,8192]{1,0:T(8,128)(2,1)} %bitcast.7, bf16[32,8192]{1,0:T(8,128)(2,1)} %bitcast.9, f32[32,32]{1,0:T(8,128)} %warm_ref.1), custom_call_target="tpu_custom_call" | custom-call | tf_op jit(solution)/shard_map/pallas_call | solution.py:218
  2.1 24.0 %all_to_all.26.refs_0_ = bf16[64,40,128]{2,1,0:T(8,128)(2,1)S(1)} all-to-all(bf16[64,40,128]{2,1,0:T(8,128)(2,1)S(1)} %shard_map.58), channel_id=1, replica_groups=mesh['gx'=8,'far'=8,'near'=2,'gz'=4] {'gx','near','gz'}, dimensions={0} | all-to-all | bytes 1310720 | tf_op jit(solution)/shard_map/all_to_all | solution.py:257
  26.1 0.3 shard_map.59
  26.4 25.6 %all_to_all.27.refs_0_ = bf16[8,32,128]{2,1,0:T(8,128)(2,1)S(1)} all-to-all(bf16[8,32,128]{2,1,0:T(8,128)(2,1)S(1)} %get-tuple-element.10), channel_id=1, replica_groups=mesh['gx'=8,'far'=8,'near'=2,'gz'=4] {'far'}, dimensions={0} | all-to-all | bytes 131072 | tf_op jit(solution)/shard_map/all_to_all | solution.py:263
  52.0 0.4 shard_map.60
  52.4 0.0 copy-start.1
  52.4 21.6 %all_to_all.28.got_ref = bf16[64,48,128]{2,1,0:T(8,128)(2,1)S(1)} all-to-all(bf16[64,48,128]{2,1,0:T(8,128)(2,1)S(1)} %shard_map.60), channel_id=1, replica_groups=mesh['gx'=8,'far'=8,'near'=2,'gz'=4] {'gx','near','gz'}, dimensions={0} | all-to-all | bytes 1572864 | tf_op jit(solution)/shard_map/all_to_all | solution.py:266
  74.0 0.0 copy-start
  74.0 1.7 %shard_map.61 = (f32[32,32]{1,0:T(8,128)}, f32[32,128]{1,0:T(8,128)S(1)}, f32[64,128]{1,0:T(8,128)}) custom-call(bf16[64,48,128]{2,1,0:T(8,128)(2,1)S(1)} %all_to_all.28.got_ref), custom_call_target="tpu_custom_call" | custom-call | tf_op jit(solution)/shard_map/pallas_call | solution.py:218
  75.7 4.6 %all-to-all-start.3 = ((f32[64,1,128]{2,1,0:T(1,128)}), f32[64,1,128]{2,1,0:T(1,128)S(1)}, u32[]{:S(2)}, u32[]{:S(2)}) async-start(f32[64,1,128]{2,1,0:T(1,128)} %bitcast.3), calls=%async_computation.3 | async-start | bytes 65536 | tf_op jit(solution)/shard_map/all_to_all | solution.py:272
  80.3 0.0 copy-done.1
  80.3 0.0 copy-done
  80.3 1.7 %shard_map.62 = (f32[32,8192]{1,0:T(8,128)S(1)}, bf16[32,8192]{1,0:T(8,128)(2,1)}) custom-call(bf16[64,48,128]{2,1,0:T(8,128)(2,1)S(1)} %all_to_all.28.got_ref, f32[32,128]{1,0:T(8,128)S(1)} %get-tuple-element.13.pair_ref, bf16[32,8192]{1,0:T(8,128)(2,1)S(1)} %bitcast.8, bf16[32,8192]{1,0:T(8,128)(2,1)S(1)} %bitcast.10), custom_call_target="tpu_custom_call" | custom-call | flops 50331648 | bytes 2621440 | tf_op jit(solution)/shard_map/pallas_call | solution.py:218
  82.0 11.8 %all-to-all-done.3 = f32[64,1,128]{2,1,0:T(1,128)S(1)} async-done(((f32[64,1,128]{2,1,0:T(1,128)}), f32[64,1,128]{2,1,0:T(1,128)S(1)}, u32[]{:S(2)}, u32[]{:S(2)}) %all-to-all-start.3) | async-done | bytes 32800 | tf_op jit(solution)/shard_map/all_to_all | solution.py:272
  93.7 1.0 %shard_map.63 = bf16[32,8192]{1,0:T(8,128)(2,1)} custom-call(f32[64,128]{1,0:T(8,128)S(1)} %bitcast.11, f32[32,8192]{1,0:T(8,128)S(1)} %get-tuple-element.14.refs_1_), custom_call_target="tpu_custom_call" | custom-call | tf_op jit(solution)/shard_map/pallas_call | solution.py:218
Async XLA Ops:
  52.4 28.0 %copy-start.1 = (bf16[1,32,8192]{2,1,0:T(8,128)(2,1)S(1)}, bf16[1,32,8192]{2,1,0:T(8,128)(2,1)}, u32[]{:S(2)}) copy-start(bf16[1,32,8192]{2,1,0:T(8,128)(2,1)} %param.4) | copy-start | bytes 1572868
  74.0 6.4 %copy-start = (bf16[1,32,8192]{2,1,0:T(8,128)(2,1)S(1)}, bf16[1,32,8192]{2,1,0:T(8,128)(2,1)}, u32[]{:S(2)}) copy-start(bf16[1,32,8192]{2,1,0:T(8,128)(2,1)} %param.3) | copy-start | bytes 1572868
  75.7 18.0 %all-to-all-start.3 = ((f32[64,1,128]{2,1,0:T(1,128)}), f32[64,1,128]{2,1,0:T(1,128)S(1)}, u32[]{:S(2)}, u32[]{:S(2)}) async-start(f32[64,1,128]{2,1,0:T(1,128)} %bitcast.3), calls=%async_computation.3 | async-start | bytes 65536 | tf_op jit(solution)/shard_map/all_to_all | solution.py:272

commit v6 on v5

--- a/solution.py
+++ b/solution.py
@@ -92,26 +92,77 @@
     return total.astype(BF16)
 
 
+def pack_gram(gram):
+    half = gram.shape[0] // 2
+    first, cross, second = gram[:half, :half], gram[:half, half:], gram[half:, half:]
+    line = lax.broadcasted_iota(jnp.int32, (half, half), 0)
+    lane = lax.broadcasted_iota(jnp.int32, (half, half), 1)
+    diagonal = jnp.sum(jnp.where(line == lane, second, 0.0), axis=1, keepdims=True)
+    return jnp.concatenate([jnp.where(line <= lane, first, second), diagonal, cross], axis=1)
+
+
+def unpack_gram(packed):
+    half = packed.shape[0]
+    line = lax.broadcasted_iota(jnp.int32, (half, half), 0)
+    lane = lax.broadcasted_iota(jnp.int32, (half, half), 1)
+    both, diagonal, cross = packed[:, :half], packed[:, half : half + 1], packed[:, half + 1 :]
+    first = jnp.where(line <= lane, both, 0.0)
+    second = jnp.where(line > lane, both, jnp.where(line == lane, diagonal, 0.0))
+    once = jnp.concatenate(
+        [
+            jnp.concatenate([first, cross], axis=1),
+            jnp.concatenate([jnp.zeros((half, half), F32), second], axis=1),
+        ],
+        axis=0,
+    )
+    line = lax.broadcasted_iota(jnp.int32, (2 * half, 2 * half), 0)
+    eye = line == lax.broadcasted_iota(jnp.int32, (2 * half, 2 * half), 1)
+    turned = lax.dot_general(
+        once,
+        eye.astype(F32),
+        (((0,), (0,)), ((), ())),
+        precision=HIGHEST,
+        preferred_element_type=F32,
+    )
+    return jnp.where(eye, once, once + turned)
+
+
 def columns_kernel(groups, got_ref, mean_ref, send_ref):
     rank, chunk = got_ref.shape[1:]
     half = rank // 2
+    replicas = send_ref.shape[0] // groups
     rows = add(got_ref)
+    across = (((1,), (1,)), ((), ()))
     product = lax.dot_general(
-        rows.astype(F32),
-        mean_ref[...],
-        (((1,), (1,)), ((), ())),
-        precision=HIGHEST,
-        preferred_element_type=F32,
-    )
+        rows.astype(F32), mean_ref[...], across, precision=HIGHEST, preferred_element_type=F32
+    )
+    gram = lax.dot_general(rows, rows, across, preferred_element_type=F32)
+    pieces = jnp.concatenate(split(pack_gram(gram), 3), axis=1)[:, : 3 * rank].astype(F32)
+    rows = rows.astype(F32)
+    share, block = rank // replicas, chunk // (half * replicas // rank)
+    lower = []
+    for replica in range(replicas):
+        mine = rows[replica * share : (replica + 1) * share]
+        mine = jnp.concatenate([mine[:, i : i + block] for i in range(0, chunk, block)], axis=0)
+        lower.append(jnp.concatenate([pieces, mine], axis=1).astype(BF16))
     width = product.shape[1] // groups
     for group in range(groups):
         high, low = split(product[:, group * width : (group + 1) * width], 2)
-        tail = jnp.concatenate([high[:half], high[half:], low[:half], low[half:]], axis=1)
-        for replica in range(send_ref.shape[0] // groups):
+        upper = jnp.concatenate([high[:half], high[half:], low[:half], low[half:]], axis=1)
+        for replica in range(replicas):
             peer = replica * groups + group
-            for i in range(chunk // LANES):
-                send_ref[peer, i * rank : (i + 1) * rank, :] = rows[:, i * LANES : (i + 1) * LANES]
-            send_ref[peer, chunk // LANES * rank :, :] = tail
+            send_ref[peer, 0:half, :] = upper
+            send_ref[peer, half:rank, :] = lower[replica]
+
+
+def share_kernel(got_ref, share_ref):
+    peers, rank, chunk = got_ref.shape
+    share = share_ref.shape[0]
+    half = rank // 2
+    for peer in range(peers):
+        mine = got_ref[peer, half:rank, 3 * rank :].astype(F32)
+        mine = jnp.concatenate([mine[i : i + share] for i in range(0, half, share)], axis=1)
+        share_ref[:, peer * chunk : (peer + 1) * chunk] = mine.astype(BF16)
 
 
 def eliminate(gram, product):
@@ -140,25 +191,18 @@
 
 
 def factor_kernel(got_ref, next_ref, pair_ref, norm_ref):
-    peers, tall, _ = got_ref.shape
     rank, width = next_ref.shape
-    high = tall - rank // 2
-    tails = [got_ref[peer, high:, :].astype(F32) for peer in range(peers)]
-    while len(tails) > 1:
-        tails = [sum(tails[i + 1 : i + 2], tails[i]) for i in range(0, len(tails), 2)]
-    tails = tails[0][:, : 2 * width] + tails[0][:, 2 * width :]
-    product = jnp.concatenate([tails[:, :width], tails[:, width:]], axis=0)
-    gram = jnp.zeros((rank, rank), F32)
-    for first in range(0, peers, 8):
-        rows = jnp.concatenate(
-            [
-                got_ref[peer, i : i + rank, :]
-                for peer in range(first, min(first + 8, peers))
-                for i in range(0, high, rank)
-            ],
-            axis=1,
-        )
-        gram += lax.dot_general(rows, rows, (((1,), (1,)), ((), ())), preferred_element_type=F32)
+    half = rank // 2
+    sums = [got_ref[peer].astype(F32) for peer in range(got_ref.shape[0])]
+    while len(sums) > 1:
+        sums = [sum(sums[i + 1 : i + 2], sums[i]) for i in range(0, len(sums), 2)]
+    upper, lower = sums[0][:half], sums[0][half:]
+    upper = upper[:, : 2 * width] + upper[:, 2 * width :]
+    product = jnp.concatenate([upper[:, :width], upper[:, width:]], axis=0)
+    third = jnp.concatenate(
+        [lower[:, 2 * rank + 2 : 3 * rank], jnp.zeros((half, 3), F32)], axis=1
+    )
+    gram = unpack_gram(lower[:, : rank + 1] + lower[:, rank + 1 : 2 * rank + 2] + third)
     line = lax.broadcasted_iota(jnp.int32, (rank, rank), 0)
     eye = (line == lax.broadcasted_iota(jnp.int32, (rank, rank), 1)).astype(F32)
     trace = jnp.sum(gram * eye)
@@ -170,12 +214,9 @@
     )
 
 
-def residual_kernel(got_ref, pair_ref, gradient_ref, error_ref, decompressed_ref, next_ref):
-    peers, tall, _ = got_ref.shape
+def residual_kernel(shares_ref, pair_ref, gradient_ref, error_ref, decompressed_ref, next_ref):
+    width, row_count = next_ref.shape
     rank = pair_ref.shape[0]
-    high = tall - rank // 2
-    chunk = high // rank * LANES
-    width = next_ref.shape[0]
     mix = lax.dot_general(
         pair_ref[:, :width],
         pair_ref[:, width : width + rank],
@@ -184,11 +225,12 @@
         preferred_element_type=F32,
     )
     mix = jnp.concatenate(split(mix, 3), axis=1)
-    for peer in range(peers):
-        part = slice(peer * chunk, (peer + 1) * chunk)
+    step = 512
+    for start in range(0, row_count, step):
+        part = slice(start, start + step)
         rows = jnp.concatenate(
-            [got_ref[peer, i : i + rank, :] for i in range(0, high, rank)], axis=1
-        )
+            [shares_ref[i, :, part].astype(F32) for i in range(shares_ref.shape[0])], axis=0
+        ).astype(BF16)
         decompressed = jnp.dot(
             mix, jnp.concatenate([rows, rows, rows], axis=0), preferred_element_type=F32
         )
@@ -261,7 +303,7 @@
         got,
     )
     got = lax.all_to_all(send, "far", 0, 0)
-    message = shape((peers, rank * chunk // LANES + rank // 2, LANES), BF16)
+    message = shape((peers, rank, LANES), BF16)
     send = call(lambda *refs: columns_kernel(groups, *refs), message, got, mean)
     got = lax.all_to_all(send, plane, 0, 0)
     next_factor, pair, norm = call(
@@ -270,10 +312,12 @@
         got,
     )
     norms = lax.all_to_all(norm, ("far", "near", "gz"), 0, 0, tiled=True)
+    share = call(share_kernel, shape((rank // replicas, row_count), BF16), got)
+    shares = lax.all_gather(share, "gx")
     decompressed, next_error = call(
         residual_kernel,
         (shape((width, row_count), F32), shape((width, row_count), BF16)),
-        got,
+        shares,
         pair,
         gradient,
         error_buffer,

time: 95 us -> 94 us (0.989)
  waiting for transfers between devices: 11.8 us -> 0.01 us
  blocking collectives: 71.2 us -> 81.6 us
    all_gather x0 -> x1, blocking collectives: none -> 13.3 us  [per_device(): shares = lax.all_gather(share, 'gx')]
    all_to_all x1, waiting for transfers between devices: 11.8 us -> 0.01 us  [per_device(): norms = lax.all_to_all(norm, ('far', 'near', 'gz'), 0, 0, tiled=True)]
    all_to_all x2, blocking collectives: 45.6 us -> 42.7 us  [per_device(): got = lax.all_to_all(send, plane, 0, 0)]
    pallas_call x6 -> x7, Pallas kernels: 6.49 us -> 6.83 us  [call(): pl.pallas_call(kernel, out_shape=outs, in_specs=[pl.BlockSpec(memory_spac...]
  transfers between devices with their start and end apart: 1 -> 1, of which waited for: 1 -> 0; matrix products, arithmetic and copies ran while one was open for 0% -> 0% of each run, Pallas kernels for 2% -> 2%
where the time goes in v6:
time: 94 us; the launch traced here: 93.7 us
  blocking collectives  81.6 us (87%)
  Pallas kernels  6.83 us (7%)
  starting transfers between devices  4.59 us (5%)
    all_to_all x2, blocking collectives, per_device(): got = lax.all_to_all(send, plane, 0, 0)  42.7 us
    all_to_all x1, blocking collectives, per_device(): got = lax.all_to_all(send, 'far', 0, 0)  25.6 us
    all_gather x1, blocking collectives, per_device(): shares = lax.all_gather(share, 'gx')  13.3 us
    pallas_call x7, Pallas kernels, call(): pl.pallas_call(kernel, out_shape=outs, in_specs=[pl.BlockSpec(memory_spac...  6.83 us
    all_to_all x1, starting transfers between devices, per_device(): norms = lax.all_to_all(norm, ('far', 'near', 'gz'), 0, 0, tiled=True)  4.59 us
  transfers between devices with their start and end apart: 1, of which 0 were waited for; matrix products, arithmetic and copies ran while one was open for 0% of the time, Pallas kernels for 2%

profile of v6, /device:TPU:1, one launch (start us, length us, event | category | flops | bytes accessed | tf_op | source)
XLA Modules:
  0.0 93.7 jit_solution(17526999895508281041)
XLA Ops:
  0.6 1.4 %shard_map.58 = bf16[64,40,128]{2,1,0:T(8,128)(2,1)S(1)} custom-call(bf16[32,8192]{1,0:T(8,128)(2,1)} %bitcast.8, bf16[32,8192]{1,0:T(8,128)(2,1)} %bitcast.10, f32[32,32]{1,0:T(8,128)} %warm_ref.1), custom_call_target="tpu_custom_call" | custom-call | tf_op jit(solution)/shard_map/pallas_call | solution.py:260
  2.1 24.0 %all_to_all.26.refs_0_ = bf16[64,40,128]{2,1,0:T(8,128)(2,1)S(1)} all-to-all(bf16[64,40,128]{2,1,0:T(8,128)(2,1)S(1)} %shard_map.58), channel_id=1, replica_groups=mesh['gx'=8,'far'=8,'near'=2,'gz'=4] {'gx','near','gz'}, dimensions={0} | all-to-all | bytes 1310720 | tf_op jit(solution)/shard_map/all_to_all | solution.py:299
  26.1 0.3 shard_map.59
  26.4 25.6 %all_to_all.27.refs_0_ = bf16[8,32,128]{2,1,0:T(8,128)(2,1)S(1)} all-to-all(bf16[8,32,128]{2,1,0:T(8,128)(2,1)S(1)} %get-tuple-element.10), channel_id=1, replica_groups=mesh['gx'=8,'far'=8,'near'=2,'gz'=4] {'far'}, dimensions={0} | all-to-all | bytes 131072 | tf_op jit(solution)/shard_map/all_to_all | solution.py:305
  52.0 0.5 shard_map.60
  52.5 18.7 %all_to_all.28.got_ref = bf16[64,32,128]{2,1,0:T(8,128)(2,1)S(1)} all-to-all(bf16[64,32,128]{2,1,0:T(8,128)(2,1)S(1)} %shard_map.60), channel_id=1, replica_groups=mesh['gx'=8,'far'=8,'near'=2,'gz'=4] {'gx','near','gz'}, dimensions={0} | all-to-all | bytes 1048576 | tf_op jit(solution)/shard_map/all_to_all | solution.py:308
  71.2 1.9 %shard_map.61 = (f32[32,32]{1,0:T(8,128)}, f32[32,128]{1,0:T(8,128)S(1)}, f32[64,128]{1,0:T(8,128)}) custom-call(bf16[64,32,128]{2,1,0:T(8,128)(2,1)S(1)} %all_to_all.28.got_ref), custom_call_target="tpu_custom_call" | custom-call | tf_op jit(solution)/shard_map/pallas_call | solution.py:260
  73.1 4.6 %all-to-all-start.3 = ((f32[64,1,128]{2,1,0:T(1,128)}), f32[64,1,128]{2,1,0:T(1,128)S(1)}, u32[]{:S(2)}, u32[]{:S(2)}) async-start(f32[64,1,128]{2,1,0:T(1,128)} %bitcast.3), calls=%async_computation.3 | async-start | bytes 65536 | tf_op jit(solution)/shard_map/all_to_all | solution.py:314
  77.7 0.0 copy-start
  77.7 0.0 copy-start.1
  77.7 0.2 shard_map.62
  77.9 13.3 %all-gather.1.shares_ref = bf16[8,4,8192]{2,1,0:T(4,128)(2,1)S(1)} all-gather(bf16[1,4,8192]{2,1,0:T(4,128)(2,1)S(1)} %bitcast.12), channel_id=2, replica_groups=mesh['gx'=8,'far'=8,'near'=2,'gz'=4] {'gx'}, dimensions={0}, use_global_device_ids=true | all-gather | bytes 589824 | tf_op jit(solution)/shard_map/all_gather | solution.py:316
  91.2 0.0 copy-done
  91.2 0.0 copy-done.1
  91.2 1.5 %shard_map.63 = (f32[32,8192]{1,0:T(8,128)S(1)}, bf16[32,8192]{1,0:T(8,128)(2,1)}) custom-call(bf16[8,4,8192]{2,1,0:T(4,128)(2,1)S(1)} %all-gather.1.shares_ref, f32[32,128]{1,0:T(8,128)S(1)} %get-tuple-element.13.pair_ref, bf16[32,8192]{1,0:T(8,128)(2,1)S(1)} %bitcast.9, bf16[32,8192]{1,0:T(8,128)(2,1)S(1)} %bitcast.11), custom_call_target="tpu_custom_call" | custom-call | flops 50331648 | bytes 2621440 | tf_op jit(solution)/shard_map/pallas_call | solution.py:260
  92.7 0.0 all-to-all-done.3
  92.7 1.0 %shard_map.64 = bf16[32,8192]{1,0:T(8,128)(2,1)} custom-call(f32[64,128]{1,0:T(8,128)S(1)} %bitcast.13, f32[32,8192]{1,0:T(8,128)S(1)} %get-tuple-element.14.refs_1_), custom_call_target="tpu_custom_call" | custom-call | tf_op jit(solution)/shard_map/pallas_call | solution.py:260
Async XLA Ops:
  73.1 19.6 %all-to-all-start.3 = ((f32[64,1,128]{2,1,0:T(1,128)}), f32[64,1,128]{2,1,0:T(1,128)S(1)}, u32[]{:S(2)}, u32[]{:S(2)}) async-start(f32[64,1,128]{2,1,0:T(1,128)} %bitcast.3), calls=%async_computation.3 | async-start | bytes 65536 | tf_op jit(solution)/shard_map/all_to_all | solution.py:314
  77.7 13.5 %copy-start = (bf16[1,32,8192]{2,1,0:T(8,128)(2,1)S(1)}, bf16[1,32,8192]{2,1,0:T(8,128)(2,1)}, u32[]{:S(2)}) copy-start(bf16[1,32,8192]{2,1,0:T(8,128)(2,1)} %param.3) | copy-start | bytes 1572868
  77.7 13.5 %copy-start.1 = (bf16[1,32,8192]{2,1,0:T(8,128)(2,1)S(1)}, bf16[1,32,8192]{2,1,0:T(8,128)(2,1)}, u32[]{:S(2)}) copy-start(bf16[1,32,8192]{2,1,0:T(8,128)(2,1)} %param.4) | copy-start | bytes 1572868

commit v7 on v6

--- a/solution.py
+++ b/solution.py
@@ -214,7 +214,9 @@
     )
 
 
-def residual_kernel(shares_ref, pair_ref, gradient_ref, error_ref, decompressed_ref, next_ref):
+def update_kernel(
+    norm_limit, norms_ref, shares_ref, pair_ref, gradient_ref, error_ref, applied_ref, next_ref, applied_tile, next_tile, sems
+):
     width, row_count = next_ref.shape
     rank = pair_ref.shape[0]
     mix = lax.dot_general(
@@ -225,32 +227,29 @@
         preferred_element_type=F32,
     )
     mix = jnp.concatenate(split(mix, 3), axis=1)
-    step = 512
-    for start in range(0, row_count, step):
-        part = slice(start, start + step)
-        rows = jnp.concatenate(
-            [shares_ref[i, :, part].astype(F32) for i in range(shares_ref.shape[0])], axis=0
-        ).astype(BF16)
-        decompressed = jnp.dot(
-            mix, jnp.concatenate([rows, rows, rows], axis=0), preferred_element_type=F32
-        )
-        decompressed_ref[:, part] = decompressed
-        tile = (gradient_ref[:, part].astype(F32) + error_ref[:, part].astype(F32)).astype(BF16)
-        next_ref[:, part] = (tile.astype(F32) - decompressed).astype(BF16)
-
-
-def clip_kernel(norm_limit, norms_ref, decompressed_ref, applied_ref, tile, sems):
-    norm_sq = jnp.sum(norms_ref[...][:, 0:1])
-    clip_scale = jnp.minimum(1.0, norm_limit * lax.rsqrt(jnp.full((1, 1), norm_sq + 1e-06, F32)))
+    norm_sq = jnp.sum(norms_ref[...][:, 0:1], axis=0, keepdims=True)
+    clip_scale = jnp.minimum(1.0, norm_limit * lax.rsqrt(norm_sq + 1e-06))
     pieces = sems.shape[0]
-    step = applied_ref.shape[1] // pieces
+    span = row_count // pieces
+    step = min(512, span)
     puts = []
     for piece in range(pieces):
-        part = pl.ds(piece * step, step)
-        tile[:, part] = (clip_scale * decompressed_ref[:, part]).astype(BF16)
-        put = pltpu.make_async_copy(tile.at[:, part], applied_ref.at[:, part], sems.at[piece])
-        put.start()
-        puts.append(put)
+        for start in range(piece * span, (piece + 1) * span, step):
+            part = slice(start, start + step)
+            rows = jnp.concatenate(
+                [shares_ref[i, :, part].astype(F32) for i in range(shares_ref.shape[0])], axis=0
+            ).astype(BF16)
+            decompressed = jnp.dot(
+                mix, jnp.concatenate([rows, rows, rows], axis=0), preferred_element_type=F32
+            )
+            applied_tile[:, part] = (clip_scale * decompressed).astype(BF16)
+            tile = (gradient_ref[:, part].astype(F32) + error_ref[:, part].astype(F32)).astype(BF16)
+            next_tile[:, part] = (tile.astype(F32) - decompressed).astype(BF16)
+        part = pl.ds(piece * span, span)
+        for i, (source, target) in enumerate(((applied_tile, applied_ref), (next_tile, next_ref))):
+            put = pltpu.make_async_copy(source.at[:, part], target.at[:, part], sems.at[piece, i])
+            put.start()
+            puts.append(put)
     for put in puts:
         put.wait()
 
@@ -314,24 +313,20 @@
     norms = lax.all_to_all(norm, ("far", "near", "gz"), 0, 0, tiled=True)
     share = call(share_kernel, shape((rank // replicas, row_count), BF16), got)
     shares = lax.all_gather(share, "gx")
-    decompressed, next_error = call(
-        residual_kernel,
-        (shape((width, row_count), F32), shape((width, row_count), BF16)),
+    applied, next_error = call(
+        lambda *refs: update_kernel(norm_limit, *refs),
+        (shape((width, row_count), BF16), shape((width, row_count), BF16)),
+        norms,
         shares,
         pair,
         gradient,
         error_buffer,
-        cost=pl.CostEstimate(
-            flops=6 * rank * width * row_count, bytes_accessed=10 * width * row_count, transcendentals=0
-        ),
-    )
-    applied = call(
-        lambda *refs: clip_kernel(norm_limit, *refs),
-        shape((width, row_count), BF16),
-        norms,
-        decompressed,
         out_space=pl.ANY,
-        scratch=[pltpu.VMEM((width, row_count), BF16), pltpu.SemaphoreType.DMA((8,))],
+        scratch=[
+            pltpu.VMEM((width, row_count), BF16),
+            pltpu.VMEM((width, row_count), BF16),
+            pltpu.SemaphoreType.DMA((4, 2)),
+        ],
     )
     return applied, next_error[None], next_factor
 

time: 94 us -> 93.1 us (level)
    pallas_call x7 -> x6, Pallas kernels: 6.83 us -> 5.91 us  [call(): pl.pallas_call(kernel, out_shape=outs, in_specs=[pl.BlockSpec(memory_spac...]
  transfers between devices with their start and end apart: 1 -> 1, of which waited for: 0 -> 0; matrix products, arithmetic and copies ran while one was open for 0% -> 0% of each run, Pallas kernels for 2% -> 0%
where the time goes in v7:
time: 93.1 us; the launch traced here: 92.8 us
  blocking collectives  81.6 us (88%)
  Pallas kernels  5.91 us (6%)
  starting transfers between devices  4.59 us (5%)
    all_to_all x2, blocking collectives, per_device(): got = lax.all_to_all(send, plane, 0, 0)  42.7 us
    all_to_all x1, blocking collectives, per_device(): got = lax.all_to_all(send, 'far', 0, 0)  25.6 us
    all_gather x1, blocking collectives, per_device(): shares = lax.all_gather(share, 'gx')  13.3 us
    pallas_call x6, Pallas kernels, call(): pl.pallas_call(kernel, out_shape=outs, in_specs=[pl.BlockSpec(memory_spac...  5.91 us
    all_to_all x1, starting transfers between devices, per_device(): norms = lax.all_to_all(norm, ('far', 'near', 'gz'), 0, 0, tiled=True)  4.59 us
  transfers between devices with their start and end apart: 1, of which 0 were waited for; matrix products, arithmetic and copies ran while one was open for 0% of the time, Pallas kernels for 0%

profile of v7, /device:TPU:1, one launch (start us, length us, event | category | flops | bytes accessed | tf_op | source)
XLA Modules:
  0.0 92.8 jit_solution(531131797733679731)
XLA Ops:
  0.6 1.4 %shard_map.58 = bf16[64,40,128]{2,1,0:T(8,128)(2,1)S(1)} custom-call(bf16[32,8192]{1,0:T(8,128)(2,1)} %bitcast.8, bf16[32,8192]{1,0:T(8,128)(2,1)} %bitcast.10, f32[32,32]{1,0:T(8,128)} %warm_ref.1), custom_call_target="tpu_custom_call" | custom-call | tf_op jit(solution)/shard_map/pallas_call | solution.py:259
  2.1 24.0 %all_to_all.26.refs_0_ = bf16[64,40,128]{2,1,0:T(8,128)(2,1)S(1)} all-to-all(bf16[64,40,128]{2,1,0:T(8,128)(2,1)S(1)} %shard_map.58), channel_id=1, replica_groups=mesh['gx'=8,'far'=8,'near'=2,'gz'=4] {'gx','near','gz'}, dimensions={0} | all-to-all | bytes 1310720 | tf_op jit(solution)/shard_map/all_to_all | solution.py:298
  26.1 0.3 shard_map.59
  26.4 25.6 %all_to_all.27.refs_0_ = bf16[8,32,128]{2,1,0:T(8,128)(2,1)S(1)} all-to-all(bf16[8,32,128]{2,1,0:T(8,128)(2,1)S(1)} %get-tuple-element.10), channel_id=1, replica_groups=mesh['gx'=8,'far'=8,'near'=2,'gz'=4] {'far'}, dimensions={0} | all-to-all | bytes 131072 | tf_op jit(solution)/shard_map/all_to_all | solution.py:304
  52.0 0.5 shard_map.60
  52.5 18.7 %all_to_all.28.got_ref = bf16[64,32,128]{2,1,0:T(8,128)(2,1)S(1)} all-to-all(bf16[64,32,128]{2,1,0:T(8,128)(2,1)S(1)} %shard_map.60), channel_id=1, replica_groups=mesh['gx'=8,'far'=8,'near'=2,'gz'=4] {'gx','near','gz'}, dimensions={0} | all-to-all | bytes 1048576 | tf_op jit(solution)/shard_map/all_to_all | solution.py:307
  71.2 1.9 %shard_map.61 = (f32[32,32]{1,0:T(8,128)}, f32[32,128]{1,0:T(8,128)S(1)}, f32[64,128]{1,0:T(8,128)}) custom-call(bf16[64,32,128]{2,1,0:T(8,128)(2,1)S(1)} %all_to_all.28.got_ref), custom_call_target="tpu_custom_call" | custom-call | tf_op jit(solution)/shard_map/pallas_call | solution.py:259
  73.1 4.6 %all-to-all-start.3 = ((f32[64,1,128]{2,1,0:T(1,128)}), f32[64,1,128]{2,1,0:T(1,128)S(1)}, u32[]{:S(2)}, u32[]{:S(2)}) async-start(f32[64,1,128]{2,1,0:T(1,128)} %bitcast.3), calls=%async_computation.3 | async-start | bytes 65536 | tf_op jit(solution)/shard_map/all_to_all | solution.py:313
  77.7 0.0 copy-start
  77.7 0.0 copy-start.1
  77.7 0.2 shard_map.62
  77.9 13.3 %all-gather.1.refs_1_ = bf16[8,4,8192]{2,1,0:T(4,128)(2,1)S(1)} all-gather(bf16[1,4,8192]{2,1,0:T(4,128)(2,1)S(1)} %bitcast.12), channel_id=2, replica_groups=mesh['gx'=8,'far'=8,'near'=2,'gz'=4] {'gx'}, dimensions={0}, use_global_device_ids=true | all-gather | bytes 589824 | tf_op jit(solution)/shard_map/all_gather | solution.py:315
  91.2 0.0 all-to-all-done.3
  91.2 0.0 copy-done
  91.2 0.0 copy-done.1
  91.3 1.6 %shard_map.63 = (bf16[32,8192]{1,0:T(8,128)(2,1)}, bf16[32,8192]{1,0:T(8,128)(2,1)}) custom-call(f32[64,128]{1,0:T(8,128)S(1)} %bitcast.13, bf16[8,4,8192]{2,1,0:T(4,128)(2,1)S(1)} %all-gather.1.refs_1_, f32[32,128]{1,0:T(8,128)S(1)} %get-tuple-element.13.refs_2_, bf16[32,8192]{1,0:T(8,128)(2,1)S(1)} %bitcast.9, bf16[32,8192]{1,0:T(8,128)(2,1)S(1)} %bitcast.11), custom_call_target="tpu_custom_call" | custom-call | tf_op jit(solution)/shard_map/pallas_call | solution.py:259
Async XLA Ops:
  73.1 18.1 %all-to-all-start.3 = ((f32[64,1,128]{2,1,0:T(1,128)}), f32[64,1,128]{2,1,0:T(1,128)S(1)}, u32[]{:S(2)}, u32[]{:S(2)}) async-start(f32[64,1,128]{2,1,0:T(1,128)} %bitcast.3), calls=%async_computation.3 | async-start | bytes 65536 | tf_op jit(solution)/shard_map/all_to_all | solution.py:313
  77.7 13.5 %copy-start = (bf16[1,32,8192]{2,1,0:T(8,128)(2,1)S(1)}, bf16[1,32,8192]{2,1,0:T(8,128)(2,1)}, u32[]{:S(2)}) copy-start(bf16[1,32,8192]{2,1,0:T(8,128)(2,1)} %param.3) | copy-start | bytes 1572868
  77.7 13.5 %copy-start.1 = (bf16[1,32,8192]{2,1,0:T(8,128)(2,1)S(1)}, bf16[1,32,8192]{2,1,0:T(8,128)(2,1)}, u32[]{:S(2)}) copy-start(bf16[1,32,8192]{2,1,0:T(8,128)(2,1)} %param.4) | copy-start | bytes 1572868

commit v8 on v7

--- a/solution.py
+++ b/solution.py
@@ -117,14 +117,7 @@
     )
     line = lax.broadcasted_iota(jnp.int32, (2 * half, 2 * half), 0)
     eye = line == lax.broadcasted_iota(jnp.int32, (2 * half, 2 * half), 1)
-    turned = lax.dot_general(
-        once,
-        eye.astype(F32),
-        (((0,), (0,)), ((), ())),
-        precision=HIGHEST,
-        preferred_element_type=F32,
-    )
-    return jnp.where(eye, once, once + turned)
+    return jnp.where(eye, once, once + once.T)
 
 
 def columns_kernel(groups, got_ref, mean_ref, send_ref):
@@ -153,16 +146,6 @@
             peer = replica * groups + group
             send_ref[peer, 0:half, :] = upper
             send_ref[peer, half:rank, :] = lower[replica]
-
-
-def share_kernel(got_ref, share_ref):
-    peers, rank, chunk = got_ref.shape
-    share = share_ref.shape[0]
-    half = rank // 2
-    for peer in range(peers):
-        mine = got_ref[peer, half:rank, 3 * rank :].astype(F32)
-        mine = jnp.concatenate([mine[i : i + share] for i in range(0, half, share)], axis=1)
-        share_ref[:, peer * chunk : (peer + 1) * chunk] = mine.astype(BF16)
 
 
 def eliminate(gram, product):
@@ -190,10 +173,16 @@
     return work[:, width : width + rank], work[:, :width]
 
 
-def factor_kernel(got_ref, next_ref, pair_ref, norm_ref):
+def factor_kernel(got_ref, next_ref, pair_ref, norm_ref, share_ref):
     rank, width = next_ref.shape
     half = rank // 2
-    sums = [got_ref[peer].astype(F32) for peer in range(got_ref.shape[0])]
+    peers, _, chunk = got_ref.shape
+    share = share_ref.shape[0]
+    for peer in range(peers):
+        mine = got_ref[peer, half:rank, 3 * rank :].astype(F32)
+        mine = jnp.concatenate([mine[i : i + share] for i in range(0, half, share)], axis=1)
+        share_ref[:, peer * chunk : (peer + 1) * chunk] = mine.astype(BF16)
+    sums = [got_ref[peer].astype(F32) for peer in range(peers)]
     while len(sums) > 1:
         sums = [sum(sums[i + 1 : i + 2], sums[i]) for i in range(0, len(sums), 2)]
     upper, lower = sums[0][:half], sums[0][half:]
@@ -305,13 +294,17 @@
     message = shape((peers, rank, LANES), BF16)
     send = call(lambda *refs: columns_kernel(groups, *refs), message, got, mean)
     got = lax.all_to_all(send, plane, 0, 0)
-    next_factor, pair, norm = call(
+    next_factor, pair, norm, share = call(
         factor_kernel,
-        (shape((rank, width), F32), shape((rank, LANES), F32), shape((columns, LANES), F32)),
+        (
+            shape((rank, width), F32),
+            shape((rank, LANES), F32),
+            shape((columns, LANES), F32),
+            shape((rank // replicas, row_count), BF16),
+        ),
         got,
     )
     norms = lax.all_to_all(norm, ("far", "near", "gz"), 0, 0, tiled=True)
-    share = call(share_kernel, shape((rank // replicas, row_count), BF16), got)
     shares = lax.all_gather(share, "gx")
     applied, next_error = call(
         lambda *refs: update_kernel(norm_limit, *refs),

time: 93.1 us -> 93 us (level)
    pallas_call x6 -> x5, Pallas kernels: 5.91 us -> 5.67 us  [call(): pl.pallas_call(kernel, out_shape=outs, in_specs=[pl.BlockSpec(memory_spac...]
  transfers between devices with their start and end apart: 1 -> 1, of which waited for: 0 -> 1; matrix products, arithmetic and copies ran while one was open for 0% -> 0% of each run, Pallas kernels for 0% -> 0%
where the time goes in v8:
time: 93 us; the launch traced here: 92.6 us
  blocking collectives  81.5 us (88%)
  Pallas kernels  5.67 us (6%)
  starting transfers between devices  4.59 us (5%)
    all_to_all x2, blocking collectives, per_device(): got = lax.all_to_all(send, plane, 0, 0)  42.7 us
    all_to_all x1, blocking collectives, per_device(): got = lax.all_to_all(send, 'far', 0, 0)  25.6 us
    all_gather x1, blocking collectives, per_device(): shares = lax.all_gather(share, 'gx')  13.2 us
    pallas_call x5, Pallas kernels, call(): pl.pallas_call(kernel, out_shape=outs, in_specs=[pl.BlockSpec(memory_spac...  5.67 us
    all_to_all x1, starting transfers between devices, per_device(): norms = lax.all_to_all(norm, ('far', 'near', 'gz'), 0, 0, tiled=True)  4.59 us
  transfers between devices with their start and end apart: 1, of which 1 were waited for; matrix products, arithmetic and copies ran while one was open for 0% of the time, Pallas kernels for 0%

profile of v8, /device:TPU:1, one launch (start us, length us, event | category | flops | bytes accessed | tf_op | source)
XLA Modules:
  0.0 92.6 jit_solution(14644105369146932550)
XLA Ops:
  0.6 1.4 %shard_map.58 = bf16[64,40,128]{2,1,0:T(8,128)(2,1)S(1)} custom-call(bf16[32,8192]{1,0:T(8,128)(2,1)} %bitcast.8, bf16[32,8192]{1,0:T(8,128)(2,1)} %bitcast.10, f32[32,32]{1,0:T(8,128)} %warm_ref.1), custom_call_target="tpu_custom_call" | custom-call | tf_op jit(solution)/shard_map/pallas_call | solution.py:248
  2.1 24.0 %all_to_all.26.refs_0_ = bf16[64,40,128]{2,1,0:T(8,128)(2,1)S(1)} all-to-all(bf16[64,40,128]{2,1,0:T(8,128)(2,1)S(1)} %shard_map.58), channel_id=1, replica_groups=mesh['gx'=8,'far'=8,'near'=2,'gz'=4] {'gx','near','gz'}, dimensions={0} | all-to-all | bytes 1310720 | tf_op jit(solution)/shard_map/all_to_all | solution.py:287
  26.1 0.3 shard_map.59
  26.4 25.6 %all_to_all.27.refs_0_ = bf16[8,32,128]{2,1,0:T(8,128)(2,1)S(1)} all-to-all(bf16[8,32,128]{2,1,0:T(8,128)(2,1)S(1)} %get-tuple-element.11), channel_id=1, replica_groups=mesh['gx'=8,'far'=8,'near'=2,'gz'=4] {'far'}, dimensions={0} | all-to-all | bytes 131072 | tf_op jit(solution)/shard_map/all_to_all | solution.py:293
  52.0 0.5 shard_map.60
  52.5 18.7 %all_to_all.28.got_ref = bf16[64,32,128]{2,1,0:T(8,128)(2,1)S(1)} all-to-all(bf16[64,32,128]{2,1,0:T(8,128)(2,1)S(1)} %shard_map.60), channel_id=1, replica_groups=mesh['gx'=8,'far'=8,'near'=2,'gz'=4] {'gx','near','gz'}, dimensions={0} | all-to-all | bytes 1048576 | tf_op jit(solution)/shard_map/all_to_all | solution.py:296
  71.2 0.0 copy-start
  71.2 0.0 copy-start.1
  71.2 1.9 %shard_map.61 = (f32[32,32]{1,0:T(8,128)}, f32[32,128]{1,0:T(8,128)S(1)}, f32[64,128]{1,0:T(8,128)}, bf16[4,8192]{1,0:T(4,128)(2,1)S(1)}) custom-call(bf16[64,32,128]{2,1,0:T(8,128)(2,1)S(1)} %all_to_all.28.got_ref), custom_call_target="tpu_custom_call" | custom-call | tf_op jit(solution)/shard_map/pallas_call | solution.py:248
  73.0 4.6 %all-to-all-start.3 = ((f32[64,1,128]{2,1,0:T(1,128)}), f32[64,1,128]{2,1,0:T(1,128)S(1)}, u32[]{:S(2)}, u32[]{:S(2)}) async-start(f32[64,1,128]{2,1,0:T(1,128)} %bitcast.3), calls=%async_computation.3 | async-start | bytes 65536 | tf_op jit(solution)/shard_map/all_to_all | solution.py:307
  77.6 13.2 %all-gather.1.refs_1_ = bf16[8,4,8192]{2,1,0:T(4,128)(2,1)S(1)} all-gather(bf16[1,4,8192]{2,1,0:T(4,128)(2,1)S(1)} %bitcast.13), channel_id=2, replica_groups=mesh['gx'=8,'far'=8,'near'=2,'gz'=4] {'gx'}, dimensions={0}, use_global_device_ids=true | all-gather | bytes 589824 | tf_op jit(solution)/shard_map/all_gather | solution.py:308
  90.8 0.2 all-to-all-done.3
  91.1 0.0 copy-done
  91.1 0.0 copy-done.1
  91.1 1.6 %shard_map.62 = (bf16[32,8192]{1,0:T(8,128)(2,1)}, bf16[32,8192]{1,0:T(8,128)(2,1)}) custom-call(f32[64,128]{1,0:T(8,128)S(1)} %bitcast.12, bf16[8,4,8192]{2,1,0:T(4,128)(2,1)S(1)} %all-gather.1.refs_1_, f32[32,128]{1,0:T(8,128)S(1)} %get-tuple-element.15.refs_2_, bf16[32,8192]{1,0:T(8,128)(2,1)S(1)} %bitcast.9, bf16[32,8192]{1,0:T(8,128)(2,1)S(1)} %bitcast.11), custom_call_target="tpu_custom_call" | custom-call | tf_op jit(solution)/shard_map/pallas_call | solution.py:248
Async XLA Ops:
  71.2 19.9 %copy-start = (bf16[1,32,8192]{2,1,0:T(8,128)(2,1)S(1)}, bf16[1,32,8192]{2,1,0:T(8,128)(2,1)}, u32[]{:S(2)}) copy-start(bf16[1,32,8192]{2,1,0:T(8,128)(2,1)} %param.3) | copy-start | bytes 1572868
  71.2 19.9 %copy-start.1 = (bf16[1,32,8192]{2,1,0:T(8,128)(2,1)S(1)}, bf16[1,32,8192]{2,1,0:T(8,128)(2,1)}, u32[]{:S(2)}) copy-start(bf16[1,32,8192]{2,1,0:T(8,128)(2,1)} %param.4) | copy-start | bytes 1572868
  73.0 18.0 %all-to-all-start.3 = ((f32[64,1,128]{2,1,0:T(1,128)}), f32[64,1,128]{2,1,0:T(1,128)S(1)}, u32[]{:S(2)}, u32[]{:S(2)}) async-start(f32[64,1,128]{2,1,0:T(1,128)} %bitcast.3), calls=%async_computation.3 | async-start | bytes 65536 | tf_op jit(solution)/shard_map/all_to_all | solution.py:307

commit v9 on v8

--- a/solution.py
+++ b/solution.py
@@ -173,7 +173,7 @@
     return work[:, width : width + rank], work[:, :width]
 
 
-def factor_kernel(got_ref, next_ref, pair_ref, norm_ref, share_ref):
+def factor_kernel(got_ref, next_ref, mix_ref, norm_ref, share_ref):
     rank, width = next_ref.shape
     half = rank // 2
     peers, _, chunk = got_ref.shape
@@ -198,24 +198,24 @@
     inverse, next_factor = eliminate(gram + (0.0001 * trace / rank) * eye, product)
     next_ref[...] = next_factor
     norm_ref[...] = jnp.full(norm_ref.shape, jnp.sum(next_factor * next_factor), F32)
-    pair_ref[...] = jnp.concatenate(
-        [next_factor, inverse, jnp.zeros((rank, LANES - width - rank), F32)], axis=1
-    )
-
-
-def update_kernel(
-    norm_limit, norms_ref, shares_ref, pair_ref, gradient_ref, error_ref, applied_ref, next_ref, applied_tile, next_tile, sems
-):
-    width, row_count = next_ref.shape
-    rank = pair_ref.shape[0]
     mix = lax.dot_general(
-        pair_ref[:, :width],
-        pair_ref[:, width : width + rank],
+        next_factor,
+        inverse,
         (((0,), (0,)), ((), ())),
         precision=HIGHEST,
         preferred_element_type=F32,
     )
-    mix = jnp.concatenate(split(mix, 3), axis=1)
+    mix_ref[...] = jnp.concatenate(
+        [*split(mix, 3), jnp.zeros((width, LANES - 3 * rank), BF16)], axis=1
+    )
+
+
+def update_kernel(
+    norm_limit, norms_ref, shares_ref, mix_ref, gradient_ref, error_ref, applied_ref, next_ref, applied_tile, next_tile, sems
+):
+    width, row_count = next_ref.shape
+    rank = shares_ref.shape[0] * shares_ref.shape[1]
+    mix = mix_ref[...][:, : 3 * rank]
     norm_sq = jnp.sum(norms_ref[...][:, 0:1], axis=0, keepdims=True)
     clip_scale = jnp.minimum(1.0, norm_limit * lax.rsqrt(norm_sq + 1e-06))
     pieces = sems.shape[0]
@@ -294,11 +294,11 @@
     message = shape((peers, rank, LANES), BF16)
     send = call(lambda *refs: columns_kernel(groups, *refs), message, got, mean)
     got = lax.all_to_all(send, plane, 0, 0)
-    next_factor, pair, norm, share = call(
+    next_factor, mix, norm, share = call(
         factor_kernel,
         (
             shape((rank, width), F32),
-            shape((rank, LANES), F32),
+            shape((width, LANES), BF16),
             shape((columns, LANES), F32),
             shape((rank // replicas, row_count), BF16),
         ),
@@ -311,14 +311,14 @@
         (shape((width, row_count), BF16), shape((width, row_count), BF16)),
         norms,
         shares,
-        pair,
+        mix,
         gradient,
         error_buffer,
         out_space=pl.ANY,
         scratch=[
             pltpu.VMEM((width, row_count), BF16),
             pltpu.VMEM((width, row_count), BF16),
-            pltpu.SemaphoreType.DMA((4, 2)),
+            pltpu.SemaphoreType.DMA((8, 2)),
         ],
     )
     return applied, next_error[None], next_factor

time: 93 us -> 92.7 us (level)
  no operation moved by 1% of the time
where the time goes in v9:
time: 92.7 us; the launch traced here: 92.4 us
  blocking collectives  81.5 us (88%)
  Pallas kernels  5.41 us (6%)
  starting transfers between devices  4.59 us (5%)
    all_to_all x2, blocking collectives, per_device(): got = lax.all_to_all(send, plane, 0, 0)  42.7 us
    all_to_all x1, blocking collectives, per_device(): got = lax.all_to_all(send, 'far', 0, 0)  25.6 us
    all_gather x1, blocking collectives, per_device(): shares = lax.all_gather(share, 'gx')  13.2 us
    pallas_call x5, Pallas kernels, call(): pl.pallas_call(kernel, out_shape=outs, in_specs=[pl.BlockSpec(memory_spac...  5.41 us
    all_to_all x1, starting transfers between devices, per_device(): norms = lax.all_to_all(norm, ('far', 'near', 'gz'), 0, 0, tiled=True)  4.59 us
  transfers between devices with their start and end apart: 1, of which 1 were waited for; matrix products, arithmetic and copies ran while one was open for 0% of the time, Pallas kernels for 0%

profile of v9, /device:TPU:1, one launch (start us, length us, event | category | flops | bytes accessed | tf_op | source)
XLA Modules:
  0.0 92.4 jit_solution(2109537432349731354)
XLA Ops:
  0.6 1.4 %shard_map.58 = bf16[64,40,128]{2,1,0:T(8,128)(2,1)S(1)} custom-call(bf16[32,8192]{1,0:T(8,128)(2,1)} %bitcast.8, bf16[32,8192]{1,0:T(8,128)(2,1)} %bitcast.10, f32[32,32]{1,0:T(8,128)} %warm_ref.1), custom_call_target="tpu_custom_call" | custom-call | tf_op jit(solution)/shard_map/pallas_call | solution.py:248
  2.1 24.0 %all_to_all.26.refs_0_ = bf16[64,40,128]{2,1,0:T(8,128)(2,1)S(1)} all-to-all(bf16[64,40,128]{2,1,0:T(8,128)(2,1)S(1)} %shard_map.58), channel_id=1, replica_groups=mesh['gx'=8,'far'=8,'near'=2,'gz'=4] {'gx','near','gz'}, dimensions={0} | all-to-all | bytes 1310720 | tf_op jit(solution)/shard_map/all_to_all | solution.py:287
  26.1 0.3 shard_map.59
  26.4 25.6 %all_to_all.27.refs_0_ = bf16[8,32,128]{2,1,0:T(8,128)(2,1)S(1)} all-to-all(bf16[8,32,128]{2,1,0:T(8,128)(2,1)S(1)} %get-tuple-element.11), channel_id=1, replica_groups=mesh['gx'=8,'far'=8,'near'=2,'gz'=4] {'far'}, dimensions={0} | all-to-all | bytes 131072 | tf_op jit(solution)/shard_map/all_to_all | solution.py:293
  52.0 0.5 shard_map.60
  52.5 18.7 %all_to_all.28.got_ref = bf16[64,32,128]{2,1,0:T(8,128)(2,1)S(1)} all-to-all(bf16[64,32,128]{2,1,0:T(8,128)(2,1)S(1)} %shard_map.60), channel_id=1, replica_groups=mesh['gx'=8,'far'=8,'near'=2,'gz'=4] {'gx','near','gz'}, dimensions={0} | all-to-all | bytes 1048576 | tf_op jit(solution)/shard_map/all_to_all | solution.py:296
  71.2 0.0 copy-start
  71.2 0.0 copy-start.1
  71.2 1.9 %shard_map.61 = (f32[32,32]{1,0:T(8,128)}, bf16[32,128]{1,0:T(8,128)(2,1)S(1)}, f32[64,128]{1,0:T(8,128)}, bf16[4,8192]{1,0:T(4,128)(2,1)S(1)}) custom-call(bf16[64,32,128]{2,1,0:T(8,128)(2,1)S(1)} %all_to_all.28.got_ref), custom_call_target="tpu_custom_call" | custom-call | tf_op jit(solution)/shard_map/pallas_call | solution.py:248
  73.1 4.6 %all-to-all-start.3 = ((f32[64,1,128]{2,1,0:T(1,128)}), f32[64,1,128]{2,1,0:T(1,128)S(1)}, u32[]{:S(2)}, u32[]{:S(2)}) async-start(f32[64,1,128]{2,1,0:T(1,128)} %bitcast.3), calls=%async_computation.3 | async-start | bytes 65536 | tf_op jit(solution)/shard_map/all_to_all | solution.py:307
  77.7 13.2 %all-gather.1.refs_1_ = bf16[8,4,8192]{2,1,0:T(4,128)(2,1)S(1)} all-gather(bf16[1,4,8192]{2,1,0:T(4,128)(2,1)S(1)} %bitcast.13), channel_id=2, replica_groups=mesh['gx'=8,'far'=8,'near'=2,'gz'=4] {'gx'}, dimensions={0}, use_global_device_ids=true | all-gather | bytes 589824 | tf_op jit(solution)/shard_map/all_gather | solution.py:308
  90.9 0.2 all-to-all-done.3
  91.1 0.0 copy-done
  91.1 0.0 copy-done.1
  91.1 1.3 %shard_map.62 = (bf16[32,8192]{1,0:T(8,128)(2,1)}, bf16[32,8192]{1,0:T(8,128)(2,1)}) custom-call(f32[64,128]{1,0:T(8,128)S(1)} %bitcast.12, bf16[8,4,8192]{2,1,0:T(4,128)(2,1)S(1)} %all-gather.1.refs_1_, bf16[32,128]{1,0:T(8,128)(2,1)S(1)} %get-tuple-element.15.refs_2_, bf16[32,8192]{1,0:T(8,128)(2,1)S(1)} %bitcast.9, bf16[32,8192]{1,0:T(8,128)(2,1)S(1)} %bitcast.11), custom_call_target="tpu_custom_call" | custom-call | tf_op jit(solution)/shard_map/pallas_call | solution.py:248
Async XLA Ops:
  71.2 19.9 %copy-start = (bf16[1,32,8192]{2,1,0:T(8,128)(2,1)S(1)}, bf16[1,32,8192]{2,1,0:T(8,128)(2,1)}, u32[]{:S(2)}) copy-start(bf16[1,32,8192]{2,1,0:T(8,128)(2,1)} %param.3) | copy-start | bytes 1572868
  71.2 19.9 %copy-start.1 = (bf16[1,32,8192]{2,1,0:T(8,128)(2,1)S(1)}, bf16[1,32,8192]{2,1,0:T(8,128)(2,1)}, u32[]{:S(2)}) copy-start(bf16[1,32,8192]{2,1,0:T(8,128)(2,1)} %param.4) | copy-start | bytes 1572868
  73.1 18.0 %all-to-all-start.3 = ((f32[64,1,128]{2,1,0:T(1,128)}), f32[64,1,128]{2,1,0:T(1,128)S(1)}, u32[]{:S(2)}, u32[]{:S(2)}) async-start(f32[64,1,128]{2,1,0:T(1,128)} %bitcast.3), calls=%async_computation.3 | async-start | bytes 65536 | tf_op jit(solution)/shard_map/all_to_all | solution.py:307

commit v10 on v9

--- a/solution.py
+++ b/solution.py
@@ -173,15 +173,13 @@
     return work[:, width : width + rank], work[:, :width]
 
 
-def factor_kernel(got_ref, next_ref, mix_ref, norm_ref, share_ref):
+def factor_kernel(
+    got_ref, next_ref, norm_ref, mix_ref, share_ref, next_tile, norm_tile, sems
+):
     rank, width = next_ref.shape
     half = rank // 2
     peers, _, chunk = got_ref.shape
     share = share_ref.shape[0]
-    for peer in range(peers):
-        mine = got_ref[peer, half:rank, 3 * rank :].astype(F32)
-        mine = jnp.concatenate([mine[i : i + share] for i in range(0, half, share)], axis=1)
-        share_ref[:, peer * chunk : (peer + 1) * chunk] = mine.astype(BF16)
     sums = [got_ref[peer].astype(F32) for peer in range(peers)]
     while len(sums) > 1:
         sums = [sum(sums[i + 1 : i + 2], sums[i]) for i in range(0, len(sums), 2)]
@@ -196,8 +194,12 @@
     eye = (line == lax.broadcasted_iota(jnp.int32, (rank, rank), 1)).astype(F32)
     trace = jnp.sum(gram * eye)
     inverse, next_factor = eliminate(gram + (0.0001 * trace / rank) * eye, product)
-    next_ref[...] = next_factor
-    norm_ref[...] = jnp.full(norm_ref.shape, jnp.sum(next_factor * next_factor), F32)
+    norm_tile[...] = jnp.full(norm_tile.shape, jnp.sum(next_factor * next_factor), F32)
+    norm_put = pltpu.make_async_copy(norm_tile, norm_ref, sems.at[0])
+    norm_put.start()
+    next_tile[...] = next_factor
+    next_put = pltpu.make_async_copy(next_tile, next_ref, sems.at[1])
+    next_put.start()
     mix = lax.dot_general(
         next_factor,
         inverse,
@@ -208,6 +210,12 @@
     mix_ref[...] = jnp.concatenate(
         [*split(mix, 3), jnp.zeros((width, LANES - 3 * rank), BF16)], axis=1
     )
+    for peer in range(peers):
+        mine = got_ref[peer, half:rank, 3 * rank :].astype(F32)
+        mine = jnp.concatenate([mine[i : i + share] for i in range(0, half, share)], axis=1)
+        share_ref[:, peer * chunk : (peer + 1) * chunk] = mine.astype(BF16)
+    norm_put.wait()
+    next_put.wait()
 
 
 def update_kernel(
@@ -249,7 +257,9 @@
         kernel,
         out_shape=outs,
         in_specs=[pl.BlockSpec(memory_space=space) for space in spaces],
-        out_specs=jax.tree.map(lambda _: pl.BlockSpec(memory_space=out_space), outs),
+        out_specs=jax.tree.map(lambda space: pl.BlockSpec(memory_space=space), out_space)
+        if isinstance(out_space, tuple)
+        else jax.tree.map(lambda _: pl.BlockSpec(memory_space=out_space), outs),
         scratch_shapes=scratch,
         compiler_params=pltpu.CompilerParams(vmem_limit_bytes=vmem * 1024 * 1024),
         cost_estimate=cost,
@@ -294,15 +304,21 @@
     message = shape((peers, rank, LANES), BF16)
     send = call(lambda *refs: columns_kernel(groups, *refs), message, got, mean)
     got = lax.all_to_all(send, plane, 0, 0)
-    next_factor, mix, norm, share = call(
+    next_factor, norm, mix, share = call(
         factor_kernel,
         (
             shape((rank, width), F32),
+            shape((columns, LANES), F32),
             shape((width, LANES), BF16),
-            shape((columns, LANES), F32),
             shape((rank // replicas, row_count), BF16),
         ),
         got,
+        out_space=(pl.ANY, pl.ANY, pltpu.VMEM, pltpu.VMEM),
+        scratch=[
+            pltpu.VMEM((rank, width), F32),
+            pltpu.VMEM((columns, LANES), F32),
+            pltpu.SemaphoreType.DMA((2,)),
+        ],
     )
     norms = lax.all_to_all(norm, ("far", "near", "gz"), 0, 0, tiled=True)
     shares = lax.all_gather(share, "gx")

time: 92.7 us -> 92.7 us (level)
  no operation moved by 1% of the time
where the time goes in v10:
time: 92.7 us; the launch traced here: 92.4 us
  blocking collectives  81.5 us (88%)
  Pallas kernels  5.41 us (6%)
  starting transfers between devices  4.6 us (5%)
    all_to_all x2, blocking collectives, per_device(): got = lax.all_to_all(send, plane, 0, 0)  42.7 us
    all_to_all x1, blocking collectives, per_device(): got = lax.all_to_all(send, 'far', 0, 0)  25.6 us
    all_gather x1, blocking collectives, per_device(): shares = lax.all_gather(share, 'gx')  13.2 us
    pallas_call x5, Pallas kernels, call(): pl.pallas_call(kernel, out_shape=outs, in_specs=[pl.BlockSpec(memory_spac...  5.41 us
    all_to_all x1, starting transfers between devices, per_device(): norms = lax.all_to_all(norm, ('far', 'near', 'gz'), 0, 0, tiled=True)  4.6 us
  transfers between devices with their start and end apart: 1, of which 1 were waited for; matrix products, arithmetic and copies ran while one was open for 0% of the time, Pallas kernels for 0%

profile of v10, /device:TPU:1, one launch (start us, length us, event | category | flops | bytes accessed | tf_op | source)
XLA Modules:
  0.0 92.4 jit_solution(1670360867614346788)
XLA Ops:
  0.6 1.4 %shard_map.58 = bf16[64,40,128]{2,1,0:T(8,128)(2,1)S(1)} custom-call(bf16[32,8192]{1,0:T(8,128)(2,1)} %bitcast.8, bf16[32,8192]{1,0:T(8,128)(2,1)} %bitcast.10, f32[32,32]{1,0:T(8,128)} %warm_ref.1), custom_call_target="tpu_custom_call" | custom-call | tf_op jit(solution)/shard_map/pallas_call | solution.py:256
  2.1 24.0 %all_to_all.26.refs_0_ = bf16[64,40,128]{2,1,0:T(8,128)(2,1)S(1)} all-to-all(bf16[64,40,128]{2,1,0:T(8,128)(2,1)S(1)} %shard_map.58), channel_id=1, replica_groups=mesh['gx'=8,'far'=8,'near'=2,'gz'=4] {'gx','near','gz'}, dimensions={0} | all-to-all | bytes 1310720 | tf_op jit(solution)/shard_map/all_to_all | solution.py:297
  26.1 0.3 shard_map.59
  26.4 25.6 %all_to_all.27.refs_0_ = bf16[8,32,128]{2,1,0:T(8,128)(2,1)S(1)} all-to-all(bf16[8,32,128]{2,1,0:T(8,128)(2,1)S(1)} %get-tuple-element.11), channel_id=1, replica_groups=mesh['gx'=8,'far'=8,'near'=2,'gz'=4] {'far'}, dimensions={0} | all-to-all | bytes 131072 | tf_op jit(solution)/shard_map/all_to_all | solution.py:303
  52.0 0.5 shard_map.60
  52.5 18.7 %all_to_all.28.got_ref = bf16[64,32,128]{2,1,0:T(8,128)(2,1)S(1)} all-to-all(bf16[64,32,128]{2,1,0:T(8,128)(2,1)S(1)} %shard_map.60), channel_id=1, replica_groups=mesh['gx'=8,'far'=8,'near'=2,'gz'=4] {'gx','near','gz'}, dimensions={0} | all-to-all | bytes 1048576 | tf_op jit(solution)/shard_map/all_to_all | solution.py:306
  71.2 0.0 copy-start
  71.2 0.0 copy-start.1
  71.2 1.9 %shard_map.61 = (f32[32,32]{1,0:T(8,128)}, f32[64,128]{1,0:T(8,128)}, bf16[32,128]{1,0:T(8,128)(2,1)S(1)}, bf16[4,8192]{1,0:T(4,128)(2,1)S(1)}) custom-call(bf16[64,32,128]{2,1,0:T(8,128)(2,1)S(1)} %all_to_all.28.got_ref), custom_call_target="tpu_custom_call" | custom-call | tf_op jit(solution)/shard_map/pallas_call | solution.py:256
  73.1 4.6 %all-to-all-start.3 = ((f32[64,1,128]{2,1,0:T(1,128)}), f32[64,1,128]{2,1,0:T(1,128)S(1)}, u32[]{:S(2)}, u32[]{:S(2)}) async-start(f32[64,1,128]{2,1,0:T(1,128)} %bitcast.3), calls=%async_computation.3 | async-start | bytes 65536 | tf_op jit(solution)/shard_map/all_to_all | solution.py:323
  77.7 13.2 %all-gather.1.refs_1_ = bf16[8,4,8192]{2,1,0:T(4,128)(2,1)S(1)} all-gather(bf16[1,4,8192]{2,1,0:T(4,128)(2,1)S(1)} %bitcast.13), channel_id=2, replica_groups=mesh['gx'=8,'far'=8,'near'=2,'gz'=4] {'gx'}, dimensions={0}, use_global_device_ids=true | all-gather | bytes 589824 | tf_op jit(solution)/shard_map/all_gather | solution.py:324
  90.9 0.2 all-to-all-done.3
  91.1 0.0 copy-done
  91.1 0.0 copy-done.1
  91.1 1.3 %shard_map.62 = (bf16[32,8192]{1,0:T(8,128)(2,1)}, bf16[32,8192]{1,0:T(8,128)(2,1)}) custom-call(f32[64,128]{1,0:T(8,128)S(1)} %bitcast.12, bf16[8,4,8192]{2,1,0:T(4,128)(2,1)S(1)} %all-gather.1.refs_1_, bf16[32,128]{1,0:T(8,128)(2,1)S(1)} %get-tuple-element.15.refs_2_, bf16[32,8192]{1,0:T(8,128)(2,1)S(1)} %bitcast.9, bf16[32,8192]{1,0:T(8,128)(2,1)S(1)} %bitcast.11), custom_call_target="tpu_custom_call" | custom-call | tf_op jit(solution)/shard_map/pallas_call | solution.py:256
Async XLA Ops:
  71.2 19.9 %copy-start = (bf16[1,32,8192]{2,1,0:T(8,128)(2,1)S(1)}, bf16[1,32,8192]{2,1,0:T(8,128)(2,1)}, u32[]{:S(2)}) copy-start(bf16[1,32,8192]{2,1,0:T(8,128)(2,1)} %param.3) | copy-start | bytes 1572868
  71.2 19.9 %copy-start.1 = (bf16[1,32,8192]{2,1,0:T(8,128)(2,1)S(1)}, bf16[1,32,8192]{2,1,0:T(8,128)(2,1)}, u32[]{:S(2)}) copy-start(bf16[1,32,8192]{2,1,0:T(8,128)(2,1)} %param.4) | copy-start | bytes 1572868
  73.1 18.1 %all-to-all-start.3 = ((f32[64,1,128]{2,1,0:T(1,128)}), f32[64,1,128]{2,1,0:T(1,128)S(1)}, u32[]{:S(2)}, u32[]{:S(2)}) async-start(f32[64,1,128]{2,1,0:T(1,128)} %bitcast.3), calls=%async_computation.3 | async-start | bytes 65536 | tf_op jit(solution)/shard_map/all_to_all | solution.py:323

commit v11 on v9

--- a/solution.py
+++ b/solution.py
@@ -78,8 +78,9 @@
         warm.append(
             jnp.concatenate([packed[:, i : i + width] for i in range(0, LANES, width)], axis=0)
         )
-    rows = jnp.dot(
-        jnp.concatenate(warm, axis=1), mean_ref[...], precision=HIGHEST, preferred_element_type=F32
+    warm = jnp.concatenate(warm, axis=1).astype(BF16)
+    rows = sum(
+        jnp.dot(warm, piece, preferred_element_type=F32) for piece in split(mean_ref[...], 3)
     ).astype(BF16)
     for peer in range(send_ref.shape[0]):
         send_ref[peer] = rows
@@ -126,8 +127,9 @@
     replicas = send_ref.shape[0] // groups
     rows = add(got_ref)
     across = (((1,), (1,)), ((), ()))
-    product = lax.dot_general(
-        rows.astype(F32), mean_ref[...], across, precision=HIGHEST, preferred_element_type=F32
+    product = sum(
+        lax.dot_general(rows, piece, across, preferred_element_type=F32)
+        for piece in split(mean_ref[...], 3)
     )
     gram = lax.dot_general(rows, rows, across, preferred_element_type=F32)
     pieces = jnp.concatenate(split(pack_gram(gram), 3), axis=1)[:, : 3 * rank].astype(F32)

time: 92.7 us -> 92.6 us (level)
  no operation moved by 1% of the time
where the time goes in v11:
time: 92.6 us; the launch traced here: 92.3 us
  blocking collectives  81.5 us (88%)
  Pallas kernels  5.3 us (6%)
  starting transfers between devices  4.59 us (5%)
    all_to_all x2, blocking collectives, per_device(): got = lax.all_to_all(send, plane, 0, 0)  42.7 us
    all_to_all x1, blocking collectives, per_device(): got = lax.all_to_all(send, 'far', 0, 0)  25.6 us
    all_gather x1, blocking collectives, per_device(): shares = lax.all_gather(share, 'gx')  13.2 us
    pallas_call x5, Pallas kernels, call(): pl.pallas_call(kernel, out_shape=outs, in_specs=[pl.BlockSpec(memory_spac...  5.3 us
    all_to_all x1, starting transfers between devices, per_device(): norms = lax.all_to_all(norm, ('far', 'near', 'gz'), 0, 0, tiled=True)  4.59 us
  transfers between devices with their start and end apart: 1, of which 1 were waited for; matrix products, arithmetic and copies ran while one was open for 0% of the time, Pallas kernels for 0%

profile of v11, /device:TPU:1, one launch (start us, length us, event | category | flops | bytes accessed | tf_op | source)
XLA Modules:
  0.0 92.3 jit_solution(8862843530203864823)
XLA Ops:
  0.6 1.4 %shard_map.58 = bf16[64,40,128]{2,1,0:T(8,128)(2,1)S(1)} custom-call(bf16[32,8192]{1,0:T(8,128)(2,1)} %bitcast.8, bf16[32,8192]{1,0:T(8,128)(2,1)} %bitcast.10, f32[32,32]{1,0:T(8,128)} %warm_ref.1), custom_call_target="tpu_custom_call" | custom-call | tf_op jit(solution)/shard_map/pallas_call | solution.py:250
  2.1 24.0 %all_to_all.26.refs_0_ = bf16[64,40,128]{2,1,0:T(8,128)(2,1)S(1)} all-to-all(bf16[64,40,128]{2,1,0:T(8,128)(2,1)S(1)} %shard_map.58), channel_id=1, replica_groups=mesh['gx'=8,'far'=8,'near'=2,'gz'=4] {'gx','near','gz'}, dimensions={0} | all-to-all | bytes 1310720 | tf_op jit(solution)/shard_map/all_to_all | solution.py:289
  26.1 0.3 shard_map.59
  26.4 25.6 %all_to_all.27.refs_0_ = bf16[8,32,128]{2,1,0:T(8,128)(2,1)S(1)} all-to-all(bf16[8,32,128]{2,1,0:T(8,128)(2,1)S(1)} %get-tuple-element.11), channel_id=1, replica_groups=mesh['gx'=8,'far'=8,'near'=2,'gz'=4] {'far'}, dimensions={0} | all-to-all | bytes 131072 | tf_op jit(solution)/shard_map/all_to_all | solution.py:295
  52.0 0.4 shard_map.60
  52.4 18.7 %all_to_all.28.got_ref = bf16[64,32,128]{2,1,0:T(8,128)(2,1)S(1)} all-to-all(bf16[64,32,128]{2,1,0:T(8,128)(2,1)S(1)} %shard_map.60), channel_id=1, replica_groups=mesh['gx'=8,'far'=8,'near'=2,'gz'=4] {'gx','near','gz'}, dimensions={0} | all-to-all | bytes 1048576 | tf_op jit(solution)/shard_map/all_to_all | solution.py:298
  71.1 0.0 copy-start
  71.1 0.0 copy-start.1
  71.1 1.9 %shard_map.61 = (f32[32,32]{1,0:T(8,128)}, bf16[32,128]{1,0:T(8,128)(2,1)S(1)}, f32[64,128]{1,0:T(8,128)}, bf16[4,8192]{1,0:T(4,128)(2,1)S(1)}) custom-call(bf16[64,32,128]{2,1,0:T(8,128)(2,1)S(1)} %all_to_all.28.got_ref), custom_call_target="tpu_custom_call" | custom-call | tf_op jit(solution)/shard_map/pallas_call | solution.py:250
  73.0 4.6 %all-to-all-start.3 = ((f32[64,1,128]{2,1,0:T(1,128)}), f32[64,1,128]{2,1,0:T(1,128)S(1)}, u32[]{:S(2)}, u32[]{:S(2)}) async-start(f32[64,1,128]{2,1,0:T(1,128)} %bitcast.3), calls=%async_computation.3 | async-start | bytes 65536 | tf_op jit(solution)/shard_map/all_to_all | solution.py:309
  77.6 13.2 %all-gather.1.refs_1_ = bf16[8,4,8192]{2,1,0:T(4,128)(2,1)S(1)} all-gather(bf16[1,4,8192]{2,1,0:T(4,128)(2,1)S(1)} %bitcast.13), channel_id=2, replica_groups=mesh['gx'=8,'far'=8,'near'=2,'gz'=4] {'gx'}, dimensions={0}, use_global_device_ids=true | all-gather | bytes 589824 | tf_op jit(solution)/shard_map/all_gather | solution.py:310
  90.8 0.2 all-to-all-done.3
  91.0 0.0 copy-done
  91.0 0.0 copy-done.1
  91.0 1.3 %shard_map.62 = (bf16[32,8192]{1,0:T(8,128)(2,1)}, bf16[32,8192]{1,0:T(8,128)(2,1)}) custom-call(f32[64,128]{1,0:T(8,128)S(1)} %bitcast.12, bf16[8,4,8192]{2,1,0:T(4,128)(2,1)S(1)} %all-gather.1.refs_1_, bf16[32,128]{1,0:T(8,128)(2,1)S(1)} %get-tuple-element.15.refs_2_, bf16[32,8192]{1,0:T(8,128)(2,1)S(1)} %bitcast.9, bf16[32,8192]{1,0:T(8,128)(2,1)S(1)} %bitcast.11), custom_call_target="tpu_custom_call" | custom-call | tf_op jit(solution)/shard_map/pallas_call | solution.py:250
Async XLA Ops:
  71.1 19.9 %copy-start = (bf16[1,32,8192]{2,1,0:T(8,128)(2,1)S(1)}, bf16[1,32,8192]{2,1,0:T(8,128)(2,1)}, u32[]{:S(2)}) copy-start(bf16[1,32,8192]{2,1,0:T(8,128)(2,1)} %param.3) | copy-start | bytes 1572868
  71.1 19.9 %copy-start.1 = (bf16[1,32,8192]{2,1,0:T(8,128)(2,1)S(1)}, bf16[1,32,8192]{2,1,0:T(8,128)(2,1)}, u32[]{:S(2)}) copy-start(bf16[1,32,8192]{2,1,0:T(8,128)(2,1)} %param.4) | copy-start | bytes 1572868
  73.0 18.0 %all-to-all-start.3 = ((f32[64,1,128]{2,1,0:T(1,128)}), f32[64,1,128]{2,1,0:T(1,128)S(1)}, u32[]{:S(2)}, u32[]{:S(2)}) async-start(f32[64,1,128]{2,1,0:T(1,128)} %bitcast.3), calls=%async_computation.3 | async-start | bytes 65536 | tf_op jit(solution)/shard_map/all_to_all | solution.py:309

commit v12 on v9

--- a/solution.py
+++ b/solution.py
@@ -266,7 +266,7 @@
     peers = replicas * groups
     chunk = row_count // peers
     norm_limit = 0.1 * math.sqrt(width * columns * row_count)
-    pieces = min(4, peers)
+    pieces = min(2, peers)
     message = shape((peers, (width * chunk + rank * width) // LANES, LANES), BF16)
 
     send = call(

time: 92.7 us -> 92.6 us (level)
  no operation moved by 1% of the time
where the time goes in v12:
time: 92.6 us; the launch traced here: 92.3 us
  blocking collectives  81.5 us (88%)
  Pallas kernels  5.29 us (6%)
  starting transfers between devices  4.59 us (5%)
    all_to_all x2, blocking collectives, per_device(): got = lax.all_to_all(send, plane, 0, 0)  42.7 us
    all_to_all x1, blocking collectives, per_device(): got = lax.all_to_all(send, 'far', 0, 0)  25.6 us
    all_gather x1, blocking collectives, per_device(): shares = lax.all_gather(share, 'gx')  13.2 us
    pallas_call x5, Pallas kernels, call(): pl.pallas_call(kernel, out_shape=outs, in_specs=[pl.BlockSpec(memory_spac...  5.29 us
    all_to_all x1, starting transfers between devices, per_device(): norms = lax.all_to_all(norm, ('far', 'near', 'gz'), 0, 0, tiled=True)  4.59 us
  transfers between devices with their start and end apart: 1, of which 1 were waited for; matrix products, arithmetic and copies ran while one was open for 0% of the time, Pallas kernels for 0%

profile of v12, /device:TPU:1, one launch (start us, length us, event | category | flops | bytes accessed | tf_op | source)
XLA Modules:
  0.0 92.3 jit_solution(17154966735886279115)
XLA Ops:
  0.6 1.3 %shard_map.58 = bf16[64,40,128]{2,1,0:T(8,128)(2,1)S(1)} custom-call(bf16[32,8192]{1,0:T(8,128)(2,1)} %bitcast.8, bf16[32,8192]{1,0:T(8,128)(2,1)} %bitcast.10, f32[32,32]{1,0:T(8,128)} %warm_ref.1), custom_call_target="tpu_custom_call" | custom-call | tf_op jit(solution)/shard_map/pallas_call | solution.py:248
  2.0 24.0 %all_to_all.26.refs_0_ = bf16[64,40,128]{2,1,0:T(8,128)(2,1)S(1)} all-to-all(bf16[64,40,128]{2,1,0:T(8,128)(2,1)S(1)} %shard_map.58), channel_id=1, replica_groups=mesh['gx'=8,'far'=8,'near'=2,'gz'=4] {'gx','near','gz'}, dimensions={0} | all-to-all | bytes 1310720 | tf_op jit(solution)/shard_map/all_to_all | solution.py:287
  26.0 0.3 shard_map.59
  26.3 25.6 %all_to_all.27.refs_0_ = bf16[8,32,128]{2,1,0:T(8,128)(2,1)S(1)} all-to-all(bf16[8,32,128]{2,1,0:T(8,128)(2,1)S(1)} %get-tuple-element.11), channel_id=1, replica_groups=mesh['gx'=8,'far'=8,'near'=2,'gz'=4] {'far'}, dimensions={0} | all-to-all | bytes 131072 | tf_op jit(solution)/shard_map/all_to_all | solution.py:293
  51.9 0.5 shard_map.60
  52.4 18.7 %all_to_all.28.got_ref = bf16[64,32,128]{2,1,0:T(8,128)(2,1)S(1)} all-to-all(bf16[64,32,128]{2,1,0:T(8,128)(2,1)S(1)} %shard_map.60), channel_id=1, replica_groups=mesh['gx'=8,'far'=8,'near'=2,'gz'=4] {'gx','near','gz'}, dimensions={0} | all-to-all | bytes 1048576 | tf_op jit(solution)/shard_map/all_to_all | solution.py:296
  71.1 0.0 copy-start
  71.1 0.0 copy-start.1
  71.1 1.9 %shard_map.61 = (f32[32,32]{1,0:T(8,128)}, bf16[32,128]{1,0:T(8,128)(2,1)S(1)}, f32[64,128]{1,0:T(8,128)}, bf16[4,8192]{1,0:T(4,128)(2,1)S(1)}) custom-call(bf16[64,32,128]{2,1,0:T(8,128)(2,1)S(1)} %all_to_all.28.got_ref), custom_call_target="tpu_custom_call" | custom-call | tf_op jit(solution)/shard_map/pallas_call | solution.py:248
  73.0 4.6 %all-to-all-start.3 = ((f32[64,1,128]{2,1,0:T(1,128)}), f32[64,1,128]{2,1,0:T(1,128)S(1)}, u32[]{:S(2)}, u32[]{:S(2)}) async-start(f32[64,1,128]{2,1,0:T(1,128)} %bitcast.3), calls=%async_computation.3 | async-start | bytes 65536 | tf_op jit(solution)/shard_map/all_to_all | solution.py:307
  77.6 13.2 %all-gather.1.refs_1_ = bf16[8,4,8192]{2,1,0:T(4,128)(2,1)S(1)} all-gather(bf16[1,4,8192]{2,1,0:T(4,128)(2,1)S(1)} %bitcast.13), channel_id=2, replica_groups=mesh['gx'=8,'far'=8,'near'=2,'gz'=4] {'gx'}, dimensions={0}, use_global_device_ids=true | all-gather | bytes 589824 | tf_op jit(solution)/shard_map/all_gather | solution.py:308
  90.7 0.2 all-to-all-done.3
  91.0 0.0 copy-done
  91.0 0.0 copy-done.1
  91.0 1.3 %shard_map.62 = (bf16[32,8192]{1,0:T(8,128)(2,1)}, bf16[32,8192]{1,0:T(8,128)(2,1)}) custom-call(f32[64,128]{1,0:T(8,128)S(1)} %bitcast.12, bf16[8,4,8192]{2,1,0:T(4,128)(2,1)S(1)} %all-gather.1.refs_1_, bf16[32,128]{1,0:T(8,128)(2,1)S(1)} %get-tuple-element.15.refs_2_, bf16[32,8192]{1,0:T(8,128)(2,1)S(1)} %bitcast.9, bf16[32,8192]{1,0:T(8,128)(2,1)S(1)} %bitcast.11), custom_call_target="tpu_custom_call" | custom-call | tf_op jit(solution)/shard_map/pallas_call | solution.py:248
Async XLA Ops:
  71.1 19.9 %copy-start = (bf16[1,32,8192]{2,1,0:T(8,128)(2,1)S(1)}, bf16[1,32,8192]{2,1,0:T(8,128)(2,1)}, u32[]{:S(2)}) copy-start(bf16[1,32,8192]{2,1,0:T(8,128)(2,1)} %param.3) | copy-start | bytes 1572868
  71.1 19.9 %copy-start.1 = (bf16[1,32,8192]{2,1,0:T(8,128)(2,1)S(1)}, bf16[1,32,8192]{2,1,0:T(8,128)(2,1)}, u32[]{:S(2)}) copy-start(bf16[1,32,8192]{2,1,0:T(8,128)(2,1)} %param.4) | copy-start | bytes 1572868
  73.0 18.0 %all-to-all-start.3 = ((f32[64,1,128]{2,1,0:T(1,128)}), f32[64,1,128]{2,1,0:T(1,128)S(1)}, u32[]{:S(2)}, u32[]{:S(2)}) async-start(f32[64,1,128]{2,1,0:T(1,128)} %bitcast.3), calls=%async_computation.3 | async-start | bytes 65536 | tf_op jit(solution)/shard_map/all_to_all | solution.py:307
